TPU v7x, 128 devices: a whole 4x4x4 slice. The times are simulated.
128 devices in a mesh: ctx: 16 (over y_hi, x, core), fsdp: 8 (over z, y_lo).
Axes of the slice: x: 4, y: 4 (y_hi: 2, y_lo: 2; y = y_hi * 2 + y_lo), z: 4, core: 2. Of those that a mesh axis runs over, the one named last changes fastest.
Arguments:
- tokens: bfloat16 [8, 2048, 1280], P('fsdp', 'ctx'), may hold values from -6 to 6
- cotangent: bfloat16 [8, 2048, 1280], P('fsdp', 'ctx'), may hold values from -6 to 6
- lengths: int32 [8, 4], P('fsdp'), may hold values from 1 to 1024, 2048 in all within a row
- block_order: int32 [8, 16], P('fsdp'), may hold values from 0 to 15, each once within a row
- w_query: bfloat16 [1280, 1280], P('fsdp'), may hold values from -0.15625 to 0.15625
- w_key: bfloat16 [1280, 1280], P('fsdp'), may hold values from -0.15625 to 0.15625
- w_value: bfloat16 [1280, 1280], P('fsdp'), may hold values from -0.15625 to 0.15625
- w_out: bfloat16 [1280, 1280], P('fsdp'), may hold values from -1.25 to 1.25
- w_up: bfloat16 [1280, 1280], P('fsdp'), may hold values from -0.15625 to 0.15625
- w_down: bfloat16 [1280, 1280], P('fsdp'), may hold values from -0.15625 to 0.15625
- g_attn: float32 [1280], replicated, may hold values from 0.1 to 1.9
- g_mlp: float32 [1280], replicated, may hold values from 0.1 to 1.9
- q_scale: float32 [80], replicated, may hold values from -1 to 1
- b_up: float32 [1280], replicated, may hold values from -3 to 3
- b_down: float32 [1280], replicated, may hold values from -3 to 3
Outputs:
- layer_out: bfloat16 [8, 2048, 1280], P('fsdp', 'ctx')
- input_grad: float32 [8, 2048, 1280], P('fsdp', 'ctx')
- grad_w_query: float32 [1280, 1280], P(('ctx', 'fsdp'))
- grad_w_key: float32 [1280, 1280], P(('ctx', 'fsdp'))
- grad_w_value: float32 [1280, 1280], P(('ctx', 'fsdp'))
- grad_w_out: float32 [1280, 1280], P(('ctx', 'fsdp'))
- grad_w_up: float32 [1280, 1280], P(('ctx', 'fsdp'))
- grad_w_down: float32 [1280, 1280], P(('ctx', 'fsdp'))
- grad_g_attn: float32 [1280], replicated
- grad_g_mlp: float32 [1280], replicated
- grad_q_scale: float32 [80], replicated
- grad_b_up: float32 [1280], replicated
- grad_b_down: float32 [1280], replicated
Inputs may be any that keep to these rules, and one draw needn't show every extreme that they name: Each row holds the 4 lengths of one group's sequences; they sum to 2048 and the longest is exactly 1024. `block_order`: each row is a permutation of the group's 16 block numbers.
All inputs are finite; a program needn't handle non-finite values.
Results may differ from a plain program's by a relative error of at most 0.015.
Values may be sent and summed in bfloat16 or wider, within the bound.
A program may use at most 192 MiB of HBM per device.

v0:
```python
import math

import jax
import jax.numpy as jnp
from jax import lax
from jax.sharding import PartitionSpec as P

HEADS = 16
HEAD_DIM = 80
BLK = 128


epsilon = 1e-06
query_const = 1.442695
masked_score = -1e30


def matmul(first_op, second_op):
    return jnp.dot(first_op, second_op, preferred_element_type=jnp.float32)


def matmul_tn(first_op, second_op):
    return lax.dot_general(
        first_op, second_op, (((0,), (0,)), ((), ())), preferred_element_type=jnp.float32
    )


def matmul_nt(first_op, second_op):
    return lax.dot_general(
        first_op, second_op, (((1,), (1,)), ((), ())), preferred_element_type=jnp.float32
    )


def rms_norm(values):
    return values * lax.rsqrt(jnp.mean(values * values, axis=-1, keepdims=True) + epsilon)


def norm_back(values, upstream, gain):
    inverse = lax.rsqrt(jnp.mean(values * values, axis=-1, keepdims=True) + epsilon)
    normed = values * inverse
    scaled = upstream * gain
    through = inverse * (scaled - normed * jnp.mean(scaled * normed, axis=-1, keepdims=True))
    return (through, jnp.sum(upstream * normed, axis=0))


def split_heads(matrix):
    return matrix.reshape(matrix.shape[0], HEADS, HEAD_DIM).transpose(1, 0, 2)


def join_heads(stacked):
    return stacked.transpose(1, 0, 2).reshape(stacked.shape[1], HEADS * HEAD_DIM)


def score_grads(allowed, query_h, keys_h, values_h, grad_h, log_h):
    scores = jnp.where(allowed, matmul_nt(query_h, keys_h), masked_score)
    probs_f = jnp.exp(scores - log_h[:, None])
    grad_probs = matmul_nt(grad_h, values_h)
    return (probs_f, grad_probs)


def on_device(
    tokens,
    cotangent,
    lengths,
    block_order,
    w_query,
    w_key,
    w_value,
    w_out,
    w_up,
    w_down,
    g_attn,
    g_mlp,
    q_scale,
    b_up,
    b_down,
):
    x_in = tokens[0].astype(jnp.float32)
    cot_bf = cotangent[0]
    row_count = x_in.shape[0]
    group_rows = row_count * lax.axis_size("ctx")
    my_start = lax.axis_index("ctx") * row_count
    slot_ids = jnp.arange(group_rows, dtype=jnp.int32)
    position = block_order[0][slot_ids // BLK] * BLK + slot_ids % BLK
    seq_ends = jnp.cumsum(lengths[0])
    seq_ids = jnp.sum((position[:, None] >= seq_ends[None, :]).astype(jnp.int32), axis=1)
    my_position = lax.dynamic_slice_in_dim(position, my_start, row_count)
    my_seq = lax.dynamic_slice_in_dim(seq_ids, my_start, row_count)
    allowed = (my_seq[:, None] == seq_ids[None, :]) & (position[None, :] <= my_position[:, None])
    wq_full, wk_full, wv_full, wo_full, wu_full, wd_full = (
        lax.all_gather(w_query, "fsdp", axis=0, tiled=True),
        lax.all_gather(w_key, "fsdp", axis=0, tiled=True),
        lax.all_gather(w_value, "fsdp", axis=0, tiled=True),
        lax.all_gather(w_out, "fsdp", axis=0, tiled=True),
        lax.all_gather(w_up, "fsdp", axis=0, tiled=True),
        lax.all_gather(w_down, "fsdp", axis=0, tiled=True),
    )
    normed = (rms_norm(x_in) * g_attn).astype(jnp.bfloat16)
    scale_vec = query_const / math.sqrt(HEAD_DIM) * jax.nn.softplus(q_scale)
    query_raw = matmul(normed, wq_full).reshape(row_count, HEADS, HEAD_DIM)
    queries = (query_raw * scale_vec).astype(jnp.bfloat16).transpose(1, 0, 2)
    key_rows = matmul(normed, wk_full).astype(jnp.bfloat16)
    value_rows = matmul(normed, wv_full).astype(jnp.bfloat16)
    keys_all, values_all = (
        lax.all_gather(key_rows, "ctx", axis=0, tiled=True),
        lax.all_gather(value_rows, "ctx", axis=0, tiled=True),
    )
    keys_heads = split_heads(keys_all)
    values_heads = split_heads(values_all)

    def attend(head_item):
        query_h, keys_h, values_h = head_item
        scores = jnp.where(allowed, matmul_nt(query_h, keys_h), masked_score)
        row_max = jnp.max(scores, axis=1, keepdims=True)
        exp_scores = jnp.exp(scores - row_max)
        row_total = jnp.sum(exp_scores, axis=1, keepdims=True)
        probabilities = (exp_scores / row_total).astype(jnp.bfloat16)
        return (matmul(probabilities, values_h), (row_max + jnp.log(row_total))[:, 0])

    head_out, log_sum = lax.map(attend, (queries, keys_heads, values_heads))
    mixed_heads = join_heads(head_out).astype(jnp.bfloat16)
    after_attn = x_in + matmul(mixed_heads, wo_full)
    normed_two = (rms_norm(after_attn) * g_mlp).astype(jnp.bfloat16)
    hidden = matmul(normed_two, wu_full) + b_up
    active = jax.nn.silu(hidden).astype(jnp.bfloat16)
    layer_out = (after_attn + matmul(active, wd_full) + b_down).astype(jnp.bfloat16)
    wq_full, wk_full, wv_full, wo_full, wu_full, wd_full = (
        lax.all_gather(w_query, "fsdp", axis=0, tiled=True),
        lax.all_gather(w_key, "fsdp", axis=0, tiled=True),
        lax.all_gather(w_value, "fsdp", axis=0, tiled=True),
        lax.all_gather(w_out, "fsdp", axis=0, tiled=True),
        lax.all_gather(w_up, "fsdp", axis=0, tiled=True),
        lax.all_gather(w_down, "fsdp", axis=0, tiled=True),
    )
    upstream = cot_bf.astype(jnp.float32)
    grad_down = matmul_tn(active, cot_bf)
    grad_bdown = jnp.sum(upstream, axis=0)
    grad_active = matmul_nt(cot_bf, wd_full)
    gate_sig = jax.nn.sigmoid(hidden)
    grad_hidden = (grad_active * gate_sig * (1.0 + hidden * (1.0 - gate_sig))).astype(jnp.bfloat16)
    grad_up = matmul_tn(normed_two, grad_hidden)
    grad_bup = jnp.sum(grad_hidden.astype(jnp.float32), axis=0)
    through_two, grad_gmlp = norm_back(after_attn, matmul_nt(grad_hidden, wu_full), g_mlp)
    grad_after = upstream + through_two
    grad_branch = grad_after.astype(jnp.bfloat16)
    grad_wout = matmul_tn(mixed_heads, grad_branch)
    grad_heads = split_heads(matmul_nt(grad_branch, wo_full).astype(jnp.bfloat16))

    def both_sides(head_item):
        query_h, keys_h, values_h, grad_h, log_h = head_item
        probs_f, grad_probs = score_grads(allowed, query_h, keys_h, values_h, grad_h, log_h)
        row_delta = jnp.sum(probs_f * grad_probs, axis=1)
        grad_scores = (probs_f * (grad_probs - row_delta[:, None])).astype(jnp.bfloat16)
        return (
            matmul(grad_scores, keys_h),
            matmul_tn(grad_scores, query_h),
            matmul_tn(probs_f.astype(jnp.bfloat16), grad_h),
        )

    grad_query_h, key_terms, value_terms = lax.map(
        both_sides, (queries, keys_heads, values_heads, grad_heads, log_sum)
    )
    key_sums, value_sums = (
        lax.psum_scatter(
            join_heads(key_terms).astype(jnp.bfloat16), "ctx", scatter_dimension=0, tiled=True
        ).astype(jnp.float32),
        lax.psum_scatter(
            join_heads(value_terms).astype(jnp.bfloat16), "ctx", scatter_dimension=0, tiled=True
        ).astype(jnp.float32),
    )
    grad_keys = key_sums.astype(jnp.bfloat16)
    grad_values = value_sums.astype(jnp.bfloat16)
    grad_query = grad_query_h.transpose(1, 0, 2)
    grad_qscale = (
        jnp.sum(grad_query * query_raw, axis=(0, 1))
        * (query_const / math.sqrt(HEAD_DIM))
        * jax.nn.sigmoid(q_scale)
    )
    grad_qraw = (grad_query * scale_vec).reshape(row_count, HEADS * HEAD_DIM).astype(jnp.bfloat16)
    grad_wq = matmul_tn(normed, grad_qraw)
    grad_wk = matmul_tn(normed, grad_keys)
    grad_wv = matmul_tn(normed, grad_values)
    grad_normed = (
        matmul_nt(grad_qraw, wq_full)
        + matmul_nt(grad_keys, wk_full)
        + matmul_nt(grad_values, wv_full)
    )
    through_one, grad_gattn = norm_back(x_in, grad_normed, g_attn)
    input_grad = (grad_after + through_one)[None]
    summed = (
        lax.psum_scatter(grad_wq, ("ctx", "fsdp"), scatter_dimension=0, tiled=True),
        lax.psum_scatter(grad_wk, ("ctx", "fsdp"), scatter_dimension=0, tiled=True),
        lax.psum_scatter(grad_wv, ("ctx", "fsdp"), scatter_dimension=0, tiled=True),
        lax.psum_scatter(grad_wout, ("ctx", "fsdp"), scatter_dimension=0, tiled=True),
        lax.psum_scatter(grad_up, ("ctx", "fsdp"), scatter_dimension=0, tiled=True),
        lax.psum_scatter(grad_down, ("ctx", "fsdp"), scatter_dimension=0, tiled=True),
    )
    small_sums = lax.psum(
        (grad_gattn, grad_gmlp, grad_qscale, grad_bup, grad_bdown), ("ctx", "fsdp")
    )
    return (
        layer_out[None],
        input_grad,
        summed[0],
        summed[1],
        summed[2],
        summed[3],
        summed[4],
        summed[5],
        small_sums[0],
        small_sums[1],
        small_sums[2],
        small_sums[3],
        small_sums[4],
    )


def solution(mesh):
    placed = (
        P("fsdp", "ctx", None),
        P("fsdp", "ctx", None),
        P("fsdp", None),
        P("fsdp", None),
        P("fsdp", None),
        P("fsdp", None),
        P("fsdp", None),
        P("fsdp", None),
        P("fsdp", None),
        P("fsdp", None),
        P(),
        P(),
        P(),
        P(),
        P(),
    )
    return jax.shard_map(
        on_device,
        mesh=mesh,
        in_specs=placed,
        out_specs=(
            P("fsdp", "ctx", None),
            P("fsdp", "ctx", None),
            P(("ctx", "fsdp"), None),
            P(("ctx", "fsdp"), None),
            P(("ctx", "fsdp"), None),
            P(("ctx", "fsdp"), None),
            P(("ctx", "fsdp"), None),
            P(("ctx", "fsdp"), None),
            P(),
            P(),
            P(),
            P(),
            P(),
        ),
        check_vma=False,
    )
```

profile of v0, /device:TPU:24, one launch (start us, length us, event | category | flops | bytes accessed | tf_op | source)
XLA Modules:
  0.0 1236.4 jit_solution(14236264217519692420)
XLA Ops:
  10.6 74.0 %all-gather.11.cloned.1.call-done = bf16[1280,1280]{1,0:T(8,128)(2,1)} async-done(((bf16[160,1280]{1,0:T(8,128)(2,1)}), bf16[1280,1280]{1,0:T(8,128)(2,1)}) %all-gather.11.cloned.1.call-update) | async-done | bytes 3276816 | tf_op jit(solution)/shard_map/all_gather | solution.py:92
  84.7 3.4 convolution_convert_fusion.2
  88.2 71.7 %all-gather.15.cloned.1.call-done = bf16[1280,1280]{1,0:T(8,128)(2,1)} async-done(((bf16[160,1280]{1,0:T(8,128)(2,1)}), bf16[1280,1280]{1,0:T(8,128)(2,1)}) %all-gather.15.cloned.1.call-update) | async-done | bytes 3276816 | tf_op jit(solution)/shard_map/all_gather | solution.py:93
  159.9 3.3 convolution_convert_fusion.1
  166.8 4.5 compare_select_fusion.1
  171.2 5.8 fusion.79
  177.3 57.9 %all-gather.9.cloned.1.call-done = bf16[1280,1280]{1,0:T(8,128)(2,1)} async-done(((bf16[160,1280]{1,0:T(8,128)(2,1)}), bf16[1280,1280]{1,0:T(8,128)(2,1)}) %all-gather.9.cloned.1.call-update) | async-done | bytes 3276816 | tf_op jit(solution)/shard_map/all_gather | solution.py:91
  235.1 5.6 copy.56
  240.8 3.0 fusion.70
  244.2 52.8 %all-gather.13.cloned.1.call-done = bf16[2048,1280]{1,0:T(8,128)(2,1)} async-done(((bf16[128,1280]{1,0:T(8,128)(2,1)}), bf16[2048,1280]{1,0:T(8,128)(2,1)}) %all-gather.13.cloned.1.call-update) | async-done | bytes 5242896 | tf_op jit(solution)/shard_map/all_gather | solution.py:105
  297.0 7.9 copy.57
  304.9 10.8 copy.60
  315.7 42.3 %all-gather.17.cloned.1.call-done = bf16[2048,1280]{1,0:T(8,128)(2,1)} async-done(((bf16[128,1280]{1,0:T(8,128)(2,1)}), bf16[2048,1280]{1,0:T(8,128)(2,1)}) %all-gather.17.cloned.1.call-update) | async-done | bytes 5242896 | tf_op jit(solution)/shard_map/all_gather | solution.py:106
  358.0 7.9 copy.58
  365.9 10.7 copy.61
  376.7 53.3 %while.30 = (s32[]{:T(128)}, bf16[16,128,80]{1,2,0:T(8,128)(2,1)S(1)}, f32[16,128]{1,0:T(8,128)S(1)}, bf16[16,128,80]{2,1,0:T(8,128)(2,1)S(1)}, bf16[16,2048,80]...) while((s32[]{:T(128)}, ...), condition=%wide.region_6.7_spmd.clone.clone, body=%wide.region_3.6_spmd.clone.sunk.clone | while | flops 86507392 | bytes 4292721 | solution.py:120
  430.0 2.8 all-gather.19.cloned.1.call-done
  432.8 2.7 multiply_reduce_fusion.3
  435.5 72.6 %all-gather.21.cloned.1.call-done = bf16[1280,1280]{1,0:T(8,128)(2,1)} async-done(((bf16[160,1280]{1,0:T(8,128)(2,1)}), bf16[1280,1280]{1,0:T(8,128)(2,1)}) %all-gather.21.cloned.1.call-update) | async-done | bytes 3276816 | tf_op jit(solution)/shard_map/all_gather | solution.py:95
  508.1 2.6 convolution_add_fusion.3
  510.6 72.6 %all-gather.23.cloned.1.call-done = bf16[1280,1280]{1,0:T(8,128)(2,1)} async-done(((bf16[160,1280]{1,0:T(8,128)(2,1)}), bf16[1280,1280]{1,0:T(8,128)(2,1)}) %all-gather.23.cloned.1.call-update) | async-done | bytes 3276816 | tf_op jit(solution)/shard_map/all_gather | solution.py:96
  583.3 3.3 convert_reduce_fusion.1
  592.5 139.8 %while.31 = (s32[]{:T(128)}, f32[16,128,80]{1,2,0:T(8,128)}, bf16[16,2048,80]{1,2,0:T(8,128)(2,1)}, bf16[16,2048,80]{1,2,0:T(8,128)(2,1)}, bf16[16,128,80]{2,1,0...) while((s32[]{:T(128)}, f32[16,128,80]{1,2,0:T(8,128)}, ...), condition=%wide.region_11.12_spmd.clone.clone, body=%wide.region_9.11_spmd.clone.sunk.clone | while | flops 212598656 | bytes 10920585 | solution.py:160
  595.7 2.0 fusion.166
  604.4 2.0 fusion.166
  613.2 2.0 fusion.166
  621.9 2.0 fusion.166
  630.6 2.0 fusion.166
  639.4 2.0 fusion.166
  656.8 2.0 fusion.166
  665.5 2.0 fusion.166
  674.3 2.0 fusion.166
  709.3 2.0 fusion.166
  726.7 2.0 fusion.166
  732.2 7.9 copy.67
  740.2 7.8 copy.69
  749.7 3.9 fusion.72
  753.6 3.7 fusion.74
  757.3 3.8 fusion.67
  761.0 3.9 fusion.84
  764.9 59.4 %reduce-scatter.7.cloned.1.call-done = bf16[128,1280]{1,0:T(8,128)(2,1)} async-done(((bf16[2048,1280]{1,0:T(8,128)(2,1)}), bf16[128,1280]{1,0:T(8,128)(2,1)}) %reduce-scatter.7.cloned.1.call-update) | async-done | bytes 327696
  824.3 4.9 fusion.87
  829.2 82.9 %reduce-scatter.9.cloned.1.call-done = bf16[128,1280]{1,0:T(8,128)(2,1)} async-done(((bf16[2048,1280]{1,0:T(8,128)(2,1)}), bf16[128,1280]{1,0:T(8,128)(2,1)}) %reduce-scatter.9.cloned.1.call-update) | async-done | bytes 327696
  912.1 4.8 fusion.85
  917.8 3.3 fusion.93
  921.2 3.5 fusion.47
  927.2 66.9 %all-reduce.6 = (f32[1280]{0:T(1024)}, f32[1280]{0:T(1024)}, f32[80]{0:T(128)}, f32[1280]{0:T(1024)}, f32[1280]{0:T(1024)}) all-reduce(f32[1280]{0:T(1024)S(1)} %get-tuple-element.262, f32[1280]{0:T(1024)S(1)} %get-tuple-element.260, f32[80]{0:T(128)S(1)} %divide_multiply_fusion, ...), channel_id=1, replica_groups=mesh['ctx'=16,'fsdp'=8] {'ctx','fsdp'}, use_global_device_ids=true, to_apply=%region_22.23 | all-reduce | flops 5200 | bytes 41600 | tf_op jit(solution)/shard_map/psum | solution.py:198
  995.3 229.7 %all-reduce.10.cloned.1.call-done = (f32[1280,1280]{1,0:T(8,128)}, f32[1280,1280]{1,0:T(8,128)}, f32[1280,1280]{1,0:T(8,128)}, f32[1280,1280]{1,0:T(8,128)}, f32[1280,1280]{1,0:T(8,128)}, /*index=5*/f32[1280,1280]{1,0:T(8,128)}) async-done(((f32[1280,1280]{1,0:T(8,128)}, f32[1280,1280]{1,0:T(8,128)}, f32[1280,1280]{1,0:T(8,128)}, f32[1280,1280]{1,0:T(8,128)}, f32[1280,1280]{1,0:T(8,128)}, ...) | async-done | bytes 39321616
  (286 shorter events, 194.8 us)
Async XLA Ops:
  7.2 152.7 %copy-start = (bf16[1,128,1280]{2,1,0:T(8,128)(2,1)S(1)}, bf16[1,128,1280]{2,1,0:T(8,128)(2,1)}, u32[]{:S(2)}) copy-start(bf16[1,128,1280]{2,1,0:T(8,128)(2,1)} %param.19) | copy-start | bytes 983044
  7.2 152.7 %copy-start.15 = (f32[1280]{0:T(1024)S(1)}, f32[1280]{0:T(1024)}, u32[]{:S(2)}) copy-start(f32[1280]{0:T(1024)} %param.29) | copy-start | bytes 15364
  7.2 77.5 %all-gather.11.cloned.1.call-start = ((), (), s32[]{:S(2)}) async-start(), calls=%async_computation.3 | async-start | bytes 3686400 | tf_op jit(solution)/shard_map/all_gather | solution.py:92
  7.9 152.0 %all-gather.15.cloned.1.call-start = ((), (), s32[]{:S(2)}) async-start(), calls=%async_computation.5 | async-start | bytes 3686400 | tf_op jit(solution)/shard_map/all_gather | solution.py:93
  8.7 226.4 %all-gather.9.cloned.1.call-start = ((), (), s32[]{:S(2)}) async-start(), calls=%async_computation.2 | async-start | bytes 3686400 | tf_op jit(solution)/shard_map/all_gather | solution.py:91
  9.4 156.4 %copy-start.21 = (f32[80]{0:T(128)S(1)}, f32[80]{0:T(128)}, u32[]{:S(2)}) copy-start(f32[80]{0:T(128)} %param.31) | copy-start | bytes 964
  9.4 156.4 %copy-start.17 = (s32[1,16]{1,0:T(1,128)S(1)}, s32[1,16]{1,0:T(1,128)}, u32[]{:S(2)}) copy-start(s32[1,16]{1,0:T(1,128)} %param.22) | copy-start | bytes 196
  9.4 157.1 %copy-start.20 = (s32[1,4]{1,0:T(1,128)S(1)}, s32[1,4]{1,0:T(1,128)}, u32[]{:S(2)}) copy-start(s32[1,4]{1,0:T(1,128)} %param.21) | copy-start | bytes 52
  9.5 287.6 %all-gather.13.cloned.1.call-start = ((), (), s32[]{:S(2)}) async-start(), calls=%async_computation.4 | async-start | bytes 5570560 | tf_op jit(solution)/shard_map/all_gather | solution.py:105
  88.1 269.9 %all-gather.17.cloned.1.call-start = ((), (), s32[]{:S(2)}) async-start(), calls=%async_computation.6 | async-start | bytes 5570560 | tf_op jit(solution)/shard_map/all_gather | solution.py:106
  163.2 269.6 %all-gather.19.cloned.1.call-start = ((), (), s32[]{:S(2)}) async-start(), calls=%async_computation.7 | async-start | bytes 3686400 | tf_op jit(solution)/shard_map/all_gather | solution.py:94
  163.8 344.3 %all-gather.21.cloned.1.call-start = ((), (), s32[]{:S(2)}) async-start(), calls=%async_computation.8 | async-start | bytes 3686400 | tf_op jit(solution)/shard_map/all_gather | solution.py:95
  164.5 418.7 %all-gather.23.cloned.1.call-start = ((), (), s32[]{:S(2)}) async-start(), calls=%async_computation.9 | async-start | bytes 3686400 | tf_op jit(solution)/shard_map/all_gather | solution.py:96
  165.3 659.0 %reduce-scatter.7.cloned.1.call-start = ((), (), s32[]{:S(2)}) async-start(), calls=%async_computation.10 | async-start | bytes 5570560
  376.7 131.4 %copy-start.16 = (f32[1280]{0:T(1024)S(1)}, f32[1280]{0:T(1024)}, u32[]{:S(2)}) copy-start(f32[1280]{0:T(1024)} %param.30) | copy-start | bytes 15364
  376.7 131.4 %copy-start.18 = (f32[1280]{0:T(1024)S(1)}, f32[1280]{0:T(1024)}, u32[]{:S(2)}) copy-start(f32[1280]{0:T(1024)} %param.32) | copy-start | bytes 15364
  430.0 78.1 %copy-start.7 = (bf16[16,128,80]{2,1,0:T(8,128)(2,1)}, bf16[16,128,80]{2,1,0:T(8,128)(2,1)S(1)}, u32[]{:S(2)}) copy-start(bf16[16,128,80]{2,1,0:T(8,128)(2,1)S(1)} %get-tuple-element.671) | copy-start | bytes 983044
  430.0 153.3 %copy-start.10 = (bf16[1,128,1280]{2,1,0:T(8,128)(2,1)S(1)}, bf16[1,128,1280]{2,1,0:T(8,128)(2,1)}, u32[]{:S(2)}) copy-start(bf16[1,128,1280]{2,1,0:T(8,128)(2,1)} %param.20) | copy-start | bytes 983044
  583.3 3.3 copy-start.3
  583.3 4.7 copy-start.11
  586.6 1.4 copy-start.13
  586.6 2.0 copy-start.2
  740.1 171.9 %reduce-scatter.9.cloned.1.call-start = ((), (), s32[]{:S(2)}) async-start(), calls=%async_computation.11 | async-start | bytes 5570560
  748.0 476.9 %all-reduce.10.cloned.1.call-start = ((), (), s32[]{:S(2)}) async-start(), calls=%async_computation.12 | async-start | bytes 78643200
  749.7 3.9 copy-start.5
  753.6 3.7 copy-start.12
  757.3 3.8 copy-start.14
  916.9 1.0 copy-start.6
  916.9 4.3 copy-start.19
  916.9 7.8 copy-start.8
  916.9 7.8 copy-start.1
  921.2 4.7 copy-start.4
  921.2 4.7 copy-start.9
Sparse Core Ops, SparseCore 0:
  9.7 74.9 all-gather.10
  86.3 73.5 all-gather.14
  161.5 73.5 all-gather.8
  238.0 58.9 all-gather.12
  299.3 58.6 all-gather.16
  359.5 73.2 all-gather.18
  434.5 73.5 all-gather.20
  509.7 73.5 all-gather.22
  740.2 84.0 reduce-scatter.6
  828.2 83.7 reduce-scatter.8
  918.5 306.3 all-reduce.9
where the time goes:
time: 1240 us
  waiting for transfers between devices  823 us (66%)
  matrix products  240 us (19%)
  local copies, waits for them, and re-layouts  68.8 us (6%)
  blocking collectives  66.9 us (5%)
  other arithmetic  22.6 us (2%)
  between operations  14.2 us (1%)
    unnamed x14, waiting for transfers between devices  376 us
    dot_general x54, matrix products, matmul_nt(): lax.dot_general(first_op, second_op, (((1,), (1,)), ((), ())), preferred_...  84.7 us
    dot_general x38, matrix products, matmul_tn(): lax.dot_general(first_op, second_op, (((0,), (0,)), ((), ())), preferred_...  80.6 us
    dot_general x38, matrix products, matmul(): return jnp.dot(first_op, second_op, preferred_element_type=jnp.float32)  74.4 us
    all_gather x1, waiting for transfers between devices, on_device(): lax.all_gather(w_key, 'fsdp', axis=0, tiled=True)  74 us
    all_gather x1, waiting for transfers between devices, on_device(): lax.all_gather(w_down, 'fsdp', axis=0, tiled=True)  72.6 us
    all_gather x1, waiting for transfers between devices, on_device(): lax.all_gather(w_up, 'fsdp', axis=0, tiled=True)  72.6 us
    all_gather x1, waiting for transfers between devices, on_device(): lax.all_gather(w_value, 'fsdp', axis=0, tiled=True)  71.7 us
  transfers between devices with their start and end apart: 11, of which 11 were waited for; matrix products, arithmetic and copies ran while one was open for 13% of the time, Pallas kernels for 0%

commit v1 on v0

v1 whole, which is shorter than its diff:
```python
import functools
import math

import jax
import jax.numpy as jnp
from jax import lax
from jax.experimental import pallas as pl
from jax.experimental.pallas import tpu as pltpu
from jax.sharding import PartitionSpec as P

D = 1280
HEADS = 16
HEAD_DIM = 80
BLK = 128
GROUP = 2048
NBLK = 16
SHARD = 160
HALF = 640
TILE = 256
WINDOW = 1024
EPS = 1e-06
QUERY_CONST = 1.442695 / math.sqrt(HEAD_DIM)
MASKED = -1e30
N_SEM = 256
MESH = pl.DeviceIdType.MESH
bf16, f32 = jnp.bfloat16, jnp.float32


def nn(a, b):
    return jnp.dot(a, b, preferred_element_type=f32)


def nt(a, b):
    return lax.dot_general(a, b, (((1,), (1,)), ((), ())), preferred_element_type=f32)


def ds(start, size, unit):
    return pl.ds(pl.multiple_of(start, unit), size)


def flip(matrix):
    return matrix.astype(f32).T.astype(matrix.dtype)


class Wire:
    def __init__(self, send_sems, recv_sems):
        self.send_sems, self.recv_sems, self.used, self.sent = send_sems, recv_sems, 0, []

    def copy(self, index, src, dst, device):
        return pltpu.make_async_remote_copy(
            src_ref=src, dst_ref=dst, send_sem=self.send_sems.at[index], recv_sem=self.recv_sems.at[index],
            device_id=device, device_id_type=MESH,
        )

    def send(self, src, dst, device):
        index = self.used
        self.used += 1
        copy = self.copy(index, src, dst, device)
        copy.start()
        self.sent.append(copy)
        return index

    def receive(self, index, ref, device):
        self.copy(index, ref, ref, device).wait_recv()

    def drain(self):
        for copy in self.sent:
            copy.wait_send()
        self.sent = []


def layer(
    lengths, order, tokens, cot, wqkv, w_out, w_up, w_down, w_query, w_key, w_value,
    g_attn, g_mlp, q_scale, b_up, b_down,
    layer_out, input_grad, grad_mlp, grad_qkv, small_out,
    later_weights,
    weights, gathered, wqkv_all, wqkv_t, raw_q, qkv_slot, qkv_pos, raw_pos, k_rows, v_rows, probs, out_pos,
    head_send, mixed_t, dout_t, dout_slot, dout_pos, dk_acc, dv_acc, grads_pos, grads_flat, grads_in,
    acts, up_in, up_all, t1, r1, t2, r2, t3, r3, swap_out, rows_out, rows_in,
    gw, gw_send, gw_in, gq_send, gq_in, ar_own, ar_one, ar_mid, ar_two,
    local_sems, send_sems, recv_sems,
):
    c, f = lax.axis_index("ctx"), lax.axis_index("fsdp")
    y_hi, x, core = c // 8, (c // 2) % 4, c % 2
    z, y_lo = f // 2, f % 2
    y = 2 * y_hi + y_lo

    def at(x_at, y_at, z_at, core_at):
        return ((y_at // 2) * 8 + x_at * 2 + core_at, z_at * 2 + y_at % 2)

    def away(dx=0, dy=0, dz=0):
        return at((x + dx) % 4, (y + dy) % 4, (z + dz) % 4, core)

    sibling = (c + 1 - 2 * core, f)
    wire = Wire(send_sems, recv_sems)

    axes = {0: "xzy", 1: "yxz", 2: "zyx"}
    here = {"x": x, "y": y, "z": z}

    def final_target(w):
        a, b, last = (here[n] for n in axes[w])
        return (4 * a + b, 2 * last + core)

    def final_source(w):
        found = dict(zip(axes[w], (c // 4, c % 4, f // 2)))
        return at(found["x"], found["y"], found["z"], f % 2)

    own_rows = ds(f * SHARD, SHARD, SHARD)
    loads = []
    for j, ref in enumerate((w_out, w_up, w_down, w_query, w_key, w_value)):
        load = pltpu.make_async_copy(ref, (weights, later_weights)[j // 3].at[j % 3, own_rows], local_sems.at[j])
        load.start()
        loads.append(load)

    barrier = pltpu.get_barrier_semaphore()
    peers = [((c + k) % 16, f) for k in range(1, 16)] + [(c, (f + k) % 8) for k in range(1, 8)]
    peers.append(at(x, 3 - y, z, core))
    for w in range(3):
        peers += [final_target(w), final_source(w)]
    for peer in peers:
        pl.semaphore_signal(barrier, inc=1, device_id=peer, device_id_type=MESH)

    x_in = tokens[...].astype(f32)
    r_one = lax.rsqrt(jnp.mean(x_in * x_in, axis=1, keepdims=True) + EPS)
    gathered[ds(c * BLK, BLK, BLK), :] = (x_in * r_one * g_attn[...]).astype(bf16)
    wqkv_all[own_rows, :] = wqkv[...]
    scale = QUERY_CONST * jnp.log(1.0 + jnp.exp(q_scale[...]))
    scale_col = jnp.broadcast_to(scale, (BLK, HEAD_DIM)).T[:, :1]

    pl.semaphore_wait(barrier, len(peers))

    def piece(yh, xa, co, part=None):
        start = ((yh * 4 + xa) * 2 + co) * BLK
        if part is None:
            return gathered.at[ds(start, BLK, BLK)]
        return gathered.at[ds(start + part * 64, 64, 64)]

    other = 1 - y_hi
    xl, xr, xo = (x + 3) % 4, (x + 1) % 4, (x + 2) % 4
    own = piece(y_hi, x, core)
    to_y = wire.send(own, own, away(dy=2))
    to_xr = wire.send(own, own, away(dx=1))
    to_xl = wire.send(own, own, away(dx=3))
    to_core = wire.send(own, own, sibling)
    cols = []
    for k in range(1, 8):
        cols.append(wire.send(wqkv_all.at[own_rows], wqkv_all.at[own_rows], (c, (f + k) % 8)))

    half_cols = ds(core * HALF, HALF, 128)
    across_y = (y + 1 + 2 * core) % 4
    from_y = (y + 3 + 2 * core) % 4

    def rows_of(buffer, zz, lo, part=None):
        start = (zz * 2 + lo) * SHARD
        if part is None:
            return buffer.at[:, ds(start, SHARD, SHARD), half_cols]
        return buffer.at[:, ds(start + part * 80, 80, 80), half_cols]

    zl, zr, zo = (z + 3) % 4, (z + 1) % 4, (z + 2) % 4

    class Gather:
        def __init__(self, buffer, own):
            self.buffer, self.own = buffer, own

        def begin(self):
            one = rows_of(self.buffer, z, y_lo)
            for load in self.own:
                load.wait()
            self.y = wire.send(one, one, at(x, across_y, z, core))
            self.r0 = wire.send(one, one, away(dz=1))
            self.l0 = wire.send(one, one, away(dz=3))
            self.kept = []

        def give(self, ref):
            self.kept.append((wire.send(ref, ref, sibling), ref))

        def second(self):
            two = rows_of(self.buffer, z, 1 - y_lo)
            wire.receive(self.y, two, at(x, from_y, z, core))
            self.r1 = wire.send(two, two, away(dz=1))
            self.l1 = wire.send(two, two, away(dz=3))
            self.give(two)

        def forward(self, lo, left, right):
            a, b = rows_of(self.buffer, zl, lo), rows_of(self.buffer, zr, lo)
            wire.receive(right, a, away(dz=3))
            ah = rows_of(self.buffer, zl, lo, 0)
            ka = wire.send(ah, ah, away(dz=1))
            self.give(a)
            wire.receive(left, b, away(dz=1))
            bh = rows_of(self.buffer, zr, lo, 1)
            kb = wire.send(bh, bh, away(dz=3))
            self.give(b)
            return ka, kb

        def third(self):
            self.f0 = self.forward(y_lo, self.l0, self.r0)

        def fourth(self):
            self.f1 = self.forward(1 - y_lo, self.l1, self.r1)

        def last(self, lo, pair):
            wire.receive(pair[0], rows_of(self.buffer, zo, lo, 0), away(dz=3))
            wire.receive(pair[1], rows_of(self.buffer, zo, lo, 1), away(dz=1))
            self.give(rows_of(self.buffer, zo, lo))

        def fifth(self):
            self.last(y_lo, self.f0)

        def sixth(self):
            self.last(1 - y_lo, self.f1)

        def finish(self):
            for index, ref in self.kept:
                wire.receive(index, ref, sibling)

    first_set, second_set = Gather(weights, loads[:3]), Gather(later_weights, loads[3:])
    first_set.begin()

    def project(yh, xa):
        chip = yh * 4 + xa
        both = nt(wqkv_t[...], gathered[ds(chip * TILE, TILE, TILE), :])
        for i in range(2):
            one = both[:, i * BLK:(i + 1) * BLK]
            raw_q[2 * chip + i] = one[:HEAD_DIM]
            qkv_slot[2 * chip + i, :HEAD_DIM] = (one[:HEAD_DIM] * scale_col).astype(bf16)
            qkv_slot[2 * chip + i, HEAD_DIM:] = one[HEAD_DIM:240].astype(bf16)

    for k, index in enumerate(cols):
        src_f = (f + 7 - k) % 8
        wire.receive(index, wqkv_all.at[ds(src_f * SHARD, SHARD, SHARD)], (c, src_f))
    wqkv_t[...] = flip(wqkv_all[...])

    def pass_on(index, ref, device):
        wire.receive(index, ref, device)
        return wire.send(ref, ref, sibling)

    wire.receive(to_core, piece(y_hi, x, 1 - core), sibling)
    project(y_hi, x)
    core_l = pass_on(to_xr, piece(y_hi, xl, core), away(dx=3))
    ring_r = wire.send(piece(y_hi, xl, core, 0), piece(y_hi, xl, core, 0), away(dx=1))
    core_r = pass_on(to_xl, piece(y_hi, xr, core), away(dx=1))
    ring_l = wire.send(piece(y_hi, xr, core, 1), piece(y_hi, xr, core, 1), away(dx=3))
    core_y = pass_on(to_y, piece(other, x, core), away(dy=2))
    y_r = wire.send(piece(other, x, core), piece(other, x, core), away(dx=1))
    y_l = wire.send(piece(other, x, core), piece(other, x, core), away(dx=3))
    first_set.second()
    wire.receive(core_l, piece(y_hi, xl, 1 - core), sibling)
    project(y_hi, xl)
    wire.receive(core_r, piece(y_hi, xr, 1 - core), sibling)
    project(y_hi, xr)
    wire.receive(core_y, piece(other, x, 1 - core), sibling)
    project(other, x)
    wire.receive(ring_r, piece(y_hi, xo, core, 0), away(dx=3))
    wire.receive(ring_l, piece(y_hi, xo, core, 1), away(dx=1))
    far = wire.send(piece(y_hi, xo, core), piece(y_hi, xo, core), away(dy=2))
    core_o = wire.send(piece(y_hi, xo, core), piece(y_hi, xo, core), sibling)
    core_yl = pass_on(y_r, piece(other, xl, core), away(dx=3))
    core_yr = pass_on(y_l, piece(other, xr, core), away(dx=1))
    first_set.third()
    wire.receive(core_o, piece(y_hi, xo, 1 - core), sibling)
    project(y_hi, xo)
    wire.receive(core_yl, piece(other, xl, 1 - core), sibling)
    project(other, xl)
    wire.receive(core_yr, piece(other, xr, 1 - core), sibling)
    project(other, xr)
    core_f = pass_on(far, piece(other, xo, core), away(dy=2))
    wire.receive(core_f, piece(other, xo, 1 - core), sibling)
    project(other, xo)

    slot_of = []
    for p in range(NBLK):
        slot = 0
        for b in range(NBLK):
            slot = jnp.where(order[0, b] == p, b, slot)
        slot_of.append(slot)
    for p in range(NBLK):
        qkv_pos[:, p * BLK:(p + 1) * BLK] = qkv_slot[slot_of[p]]
        raw_pos[:, p * BLK:(p + 1) * BLK] = raw_q[slot_of[p]]
    k_rows[...] = flip(qkv_pos[HEAD_DIM:2 * HEAD_DIM, :])
    v_rows[...] = flip(qkv_pos[2 * HEAD_DIM:, :])

    ends, total = [], 0
    for s in range(4):
        total = total + lengths[0, s]
        ends.append(total)

    at_part = 0
    parts_of = []
    for t in range(GROUP // TILE):
        low, high = max(0, t * TILE - WINDOW), (t + 1) * TILE
        width = high - low
        tile = slice(t * TILE, high)
        scores = nn(k_rows[low:high, :], qkv_pos[:HEAD_DIM, tile])
        at_q = t * TILE + lax.broadcasted_iota(jnp.int32, (1, TILE), 1)
        start = jnp.zeros((1, TILE), jnp.int32)
        for end in ends:
            start = jnp.where(at_q >= end, end, start)
        at_k = low + lax.broadcasted_iota(jnp.int32, (width, TILE), 0)
        scores = jnp.where((at_k <= at_q) & (at_k >= start), scores, MASKED)
        top = jnp.max(scores, axis=0, keepdims=True)
        powers = jnp.exp(scores - top)
        part = powers * (1.0 / jnp.sum(powers, axis=0, keepdims=True))
        part = part.astype(bf16)
        parts_of.append(slice(at_part, at_part + width))
        at_part += width
        probs[parts_of[t], :] = part
        out = nn(qkv_pos[2 * HEAD_DIM:, low:high], part).astype(bf16)
        out_pos[2 * t] = out[:, :BLK]
        out_pos[2 * t + 1] = out[:, BLK:]

    for b in range(NBLK):
        head_send[b] = out_pos[order[0, b]]

    def exchange(src_of, dst):
        return [wire.send(src_of((c + k) % 16), dst, ((c + k) % 16, f)) for k in range(1, 16)]

    def arrive(indices, dst_of):
        for k, index in enumerate(indices):
            src = (c + 15 - k) % 16
            wire.receive(index, dst_of(src), (src, f))

    head_rows = ds(c * HEAD_DIM, HEAD_DIM, HEAD_DIM)
    mixing = exchange(lambda b: head_send.at[b], mixed_t.at[head_rows])
    mixed_t[head_rows, :] = head_send[c]
    first_set.fourth()
    first_set.fifth()
    first_set.sixth()
    first_set.finish()
    wire.set_one = len(wire.sent)
    second_set.begin()

    cot_f = cot[...].astype(f32)

    def spread(a, w):
        return jnp.concatenate([nn(a, weights[w, :, n:n + 256]) for n in range(0, D, 256)], axis=1)

    def spread_back(a, w):
        return jnp.concatenate([nt(a, weights[w, n:n + 256, :]) for n in range(0, D, 256)], axis=1)

    grad_active = spread_back(cot[...], 2)
    arrive(mixing, lambda src: mixed_t.at[ds(src * HEAD_DIM, HEAD_DIM, HEAD_DIM)])

    mixed = flip(mixed_t[...])
    after = x_in + spread(mixed, 0)
    r_two = lax.rsqrt(jnp.mean(after * after, axis=1, keepdims=True) + EPS)
    n_two = after * r_two
    normed_two = (n_two * g_mlp[...]).astype(bf16)
    hidden = spread(normed_two, 1) + b_up[...]
    gate = jax.nn.sigmoid(hidden)
    active = (hidden * gate).astype(bf16)
    grad_hidden = (grad_active * gate * (1.0 + hidden * (1.0 - gate))).astype(bf16)
    back_two = spread_back(grad_hidden, 1)
    scaled = back_two * g_mlp[...]
    grad_after = cot_f + r_two * (scaled - n_two * jnp.mean(scaled * n_two, axis=1, keepdims=True))
    grad_branch = grad_after.astype(bf16)
    dout_t[...] = flip(spread_back(grad_branch, 0).astype(bf16))
    douts = exchange(lambda b: dout_t.at[ds(b * HEAD_DIM, HEAD_DIM, HEAD_DIM)], dout_slot.at[c])
    dout_slot[c] = dout_t[head_rows, :]

    my_lanes = ds(core * BLK, BLK, BLK)
    other_half = ds((1 - core) * HALF, HALF, 128)
    ups = (grad_branch, grad_hidden, cot[...])
    acts[0, :, my_lanes] = mixed_t[...]
    acts[1, :, my_lanes] = flip(normed_two)
    acts[2, :, my_lanes] = flip(active)
    for w in range(3):
        up_in[w] = ups[w]
    give_acts = wire.send(acts.at[:, :, my_lanes], acts.at[:, :, my_lanes], sibling)
    give_up = wire.send(up_in.at[:, :, other_half], up_all.at[:, my_lanes], sibling)
    for w in range(3):
        up_all[w, my_lanes, :] = up_in[w, :, half_cols]
    layer_out[...] = (after + spread(active, 2) + b_down[...]).astype(bf16)
    input_grad[...] = grad_after
    ar_own[...] = jnp.zeros_like(ar_own)
    ar_own[1:2, :] = jnp.sum(back_two * n_two, axis=0, keepdims=True)
    ar_own[2:3, :] = jnp.sum(grad_hidden.astype(f32), axis=0, keepdims=True)
    ar_own[3:4, :] = jnp.sum(cot_f, axis=0, keepdims=True)

    second_set.second()
    sib_lanes = ds((1 - core) * BLK, BLK, BLK)
    wire.receive(give_acts, acts.at[:, :, sib_lanes], sibling)
    wire.receive(give_up, up_all.at[:, sib_lanes], sibling)

    def scatter(w, stage, src_of, dst_of):
        axis = axes[w][stage]
        return [
            wire.send(src_of((here[axis] + k) % 4), dst_of(k - 1), away(**{"d" + axis: k})) for k in range(1, 4)
        ]

    def gathered_sum(w, stage, indices, first, buffers):
        axis = axes[w][stage]
        for k, index in enumerate(indices):
            wire.receive(index, buffers.at[w, k], away(**{"d" + axis: 3 - k}))
        return first.astype(f32) + buffers[w, 0].astype(f32) + buffers[w, 1].astype(f32) + buffers[w, 2].astype(f32)

    stage_one, stage_two, stage_three = {}, {}, {}
    for w in (2, 1, 0):
        for n in range(0, D, 320):
            rows = slice(n, n + 320)
            t1[w, rows, :] = nn(acts[w, rows, :], up_all[w]).astype(bf16)
        stage_one[w] = scatter(w, 0, lambda d: t1.at[w, ds(d * 320, 320, 320)], lambda k: r1.at[w, k])

    def second_stage(w):
        mine = t1[w, ds(here[axes[w][0]] * 320, 320, 320), :]
        t2[w] = gathered_sum(w, 0, stage_one[w], mine, r1).astype(bf16)
        stage_two[w] = scatter(w, 1, lambda d: t2.at[w, ds(d * 80, 80, 80)], lambda k: r2.at[w, k])

    def third_stage(w):
        mine = t2[w, ds(here[axes[w][1]] * 80, 80, 80), :]
        both = gathered_sum(w, 1, stage_two[w], mine, r2)
        for d in range(4):
            t3[w, d] = jnp.concatenate([both[20 * d:20 * d + 20], jnp.zeros((12, HALF), f32)], axis=0).astype(bf16)
        stage_three[w] = scatter(w, 2, lambda d: t3.at[w, d], lambda k: r3.at[w, k])

    def fourth_stage(w):
        both = gathered_sum(w, 2, stage_three[w], t3[w, here[axes[w][2]]], r3)
        for i in range(2):
            swap_out[w, i] = jnp.concatenate([both[10 * i:10 * i + 10], jnp.zeros((6, HALF), f32)], axis=0)
        rows_out[w, :, half_cols] = swap_out[w, core]
        return wire.send(swap_out.at[w, 1 - core], rows_out.at[w, :, half_cols], sibling)

    arrive(douts, lambda src: dout_slot.at[src])

    for p in range(NBLK):
        dout_pos[:, p * BLK:(p + 1) * BLK] = dout_slot[slot_of[p]]
    dk_acc[...] = jnp.zeros_like(dk_acc)
    dv_acc[...] = jnp.zeros_like(dv_acc)
    scale_terms = jnp.zeros((HEAD_DIM, 1), f32)
    for t in range(GROUP // TILE):
        low, high = max(0, t * TILE - WINDOW), (t + 1) * TILE
        width = high - low
        tile = slice(t * TILE, high)
        d_out = dout_pos[:, tile]
        delta = jnp.sum(d_out.astype(f32) * jnp.concatenate([out_pos[2 * t], out_pos[2 * t + 1]], axis=1).astype(f32), axis=0, keepdims=True)
        part = probs[parts_of[t], :]
        d_probs = nn(v_rows[low:high, :], d_out)
        d_scores = (part.astype(f32) * (d_probs - delta)).astype(bf16)
        dq = nn(qkv_pos[HEAD_DIM:2 * HEAD_DIM, low:high], d_scores)
        scale_terms = scale_terms + jnp.sum(dq * raw_pos[:, tile], axis=1, keepdims=True)
        dq = (dq * scale_col).astype(bf16)
        grads_pos[2 * t, :HEAD_DIM] = dq[:, :BLK]
        grads_pos[2 * t + 1, :HEAD_DIM] = dq[:, BLK:]
        dk_acc[:, low:high] += nt(qkv_pos[:HEAD_DIM, tile], d_scores)
        dv_acc[:, low:high] += nt(d_out, part)

    for p in range(NBLK):
        lanes = slice(p * BLK, (p + 1) * BLK)
        grads_pos[p, HEAD_DIM:2 * HEAD_DIM] = dk_acc[:, lanes].astype(bf16)
        grads_pos[p, 2 * HEAD_DIM:] = dv_acc[:, lanes].astype(bf16)
    for b in range(NBLK):
        block = grads_pos[order[0, b]]
        qkv_slot[b] = block
        grads_flat[:, b * BLK:(b + 1) * BLK] = block
    sent_grads = exchange(lambda b: qkv_slot.at[b], grads_in.at[c])
    grads_in[c] = qkv_slot[c]

    second_set.third()
    second_set.fourth()

    for n in range(0, D, 256):
        grad_t = nn(grads_flat[...], gathered[:, n:n + 256])
        gw[n:n + 256, :] = jnp.concatenate([grad_t, jnp.zeros((16, 256), f32)], axis=0).T
    for fs in range(8):
        picked = [gw[cs * 80 + fs * 10:cs * 80 + fs * 10 + 10, :] for cs in range(16)]
        gw_send[fs] = jnp.concatenate(picked, axis=0).astype(bf16)
    shares = [wire.send(gw_send.at[(f + k) % 8], gw_in.at[k - 1], (c, (f + k) % 8)) for k in range(1, 8)]

    for w in (2, 1, 0):
        second_stage(w)
    second_set.fifth()
    second_set.sixth()
    second_set.finish()
    for w in (2, 1, 0):
        third_stage(w)

    for copy in wire.sent[:wire.set_one]:
        copy.wait_send()
    wire.sent = wire.sent[wire.set_one:]
    loads = []
    for j in range(3):
        load = pltpu.make_async_copy(later_weights.at[j], weights.at[j], local_sems.at[j])
        load.start()
        loads.append(load)
    arrive(sent_grads, lambda src: grads_in.at[src])
    grad_normed = jnp.zeros((BLK, D), f32)
    for j in range(3):
        loads[j].wait()
        rows = slice(j * HEAD_DIM, (j + 1) * HEAD_DIM)
        joined = jnp.concatenate([grads_in[h, rows] for h in range(HEADS)], axis=0)
        grad_normed = grad_normed + spread_back(flip(joined), j)
    n_one = x_in * r_one
    scaled = grad_normed * g_attn[...]
    through = r_one * (scaled - n_one * jnp.mean(scaled * n_one, axis=1, keepdims=True))
    input_grad[...] = input_grad[...] + through
    ar_own[0:1, :] = jnp.sum(grad_normed * n_one, axis=0, keepdims=True)
    ar_own[4:5, :HEAD_DIM] = jnp.broadcast_to(scale_terms, (HEAD_DIM, BLK)).T[:1]
    ar_one[c] = ar_own[...]
    sums = exchange(lambda b: ar_own, ar_one.at[c])

    swaps = [(w, fourth_stage(w)) for w in (2, 1, 0)]
    for k, index in enumerate(shares):
        src_f = (f + 7 - k) % 8
        wire.receive(index, gw_in.at[k], (c, src_f))
    both = gw_send[f].astype(f32)
    for k in range(7):
        both = both + gw_in[k].astype(f32)
    for cs in range(16):
        gq_send[cs] = jnp.concatenate([both[10 * cs:10 * cs + 10], jnp.zeros((6, 256), f32)], axis=0).astype(bf16)
    gq_in[c] = gq_send[c]
    heads = exchange(lambda b: gq_send.at[b], gq_in.at[c])

    finals = []
    for w, index in swaps:
        wire.receive(index, rows_out.at[w, :, other_half], sibling)
        target = final_target(w)
        index = wire.used
        wire.used += 1
        stays = (target[0] == c) & (target[1] == f)
        copy = wire.copy(index, rows_out.at[w], rows_in.at[w], target)
        within = pltpu.make_async_copy(rows_out.at[w], rows_in.at[w], recv_sems.at[index])
        pl.when(jnp.logical_not(stays))(copy.start)
        pl.when(stays)(within.start)
        finals.append((w, index, copy, stays))

    arrive(sums, lambda src: ar_one.at[src])
    total_small = ar_one[0]
    for k in range(1, 16):
        total_small = total_small + ar_one[k]
    ar_mid[...] = total_small
    ar_two[f] = total_small
    sums = [wire.send(ar_mid, ar_two.at[f], (c, (f + k) % 8)) for k in range(1, 8)]
    for k, index in enumerate(sums):
        src_f = (f + 7 - k) % 8
        wire.receive(index, ar_two.at[src_f], (c, src_f))
    total_small = ar_two[0]
    for k in range(1, 8):
        total_small = total_small + ar_two[k]
    small_out[...] = total_small

    arrive(heads, lambda src: gq_in.at[src])
    grad_qkv[...] = gq_in[...]
    for w, index, copy, stays in finals:
        wire.receive(index, rows_in.at[w], final_source(w))
        pl.when(jnp.logical_not(stays))(copy.wait_send)
    grad_mlp[...] = rows_in[...]
    wire.drain()
    assert wire.used <= N_SEM


def on_device(
    tokens, cotangent, lengths, block_order, w_query, w_key, w_value, w_out, w_up, w_down,
    g_attn, g_mlp, q_scale, b_up, b_down,
):
    first = lax.axis_index("ctx") * HEAD_DIM
    columns = [lax.dynamic_slice(w, (0, first), (SHARD, HEAD_DIM)) for w in (w_query, w_key, w_value)]
    wqkv = jnp.concatenate(columns + [jnp.zeros((SHARD, 16), bf16)], axis=1)
    vmem, smem, any_space = (pl.BlockSpec(memory_space=s) for s in (pltpu.VMEM, pltpu.SMEM, pl.ANY))
    shapes = {
        "weights": ((3, D, D), bf16), "gathered": ((GROUP, D), bf16), "wqkv_all": ((D, 256), bf16),
        "wqkv_t": ((256, D), bf16), "raw_q": ((NBLK, HEAD_DIM, BLK), f32), "qkv_slot": ((NBLK, 240, BLK), bf16),
        "qkv_pos": ((240, GROUP), bf16), "raw_pos": ((HEAD_DIM, GROUP), f32), "k_rows": ((GROUP, HEAD_DIM), bf16),
        "v_rows": ((GROUP, HEAD_DIM), bf16), "probs": ((7680, TILE), bf16), "out_pos": ((NBLK, HEAD_DIM, BLK), bf16),
        "head_send": ((NBLK, HEAD_DIM, BLK), bf16), "mixed_t": ((D, BLK), bf16), "dout_t": ((D, BLK), bf16),
        "dout_slot": ((NBLK, HEAD_DIM, BLK), bf16), "dout_pos": ((HEAD_DIM, GROUP), bf16),
        "dk_acc": ((HEAD_DIM, GROUP), f32), "dv_acc": ((HEAD_DIM, GROUP), f32), "grads_pos": ((NBLK, 240, BLK), bf16),
        "grads_flat": ((240, GROUP), bf16), "grads_in": ((NBLK, 240, BLK), bf16),
        "acts": ((3, D, 2 * BLK), bf16), "up_in": ((3, BLK, D), bf16), "up_all": ((3, 2 * BLK, HALF), bf16),
        "t1": ((3, D, HALF), bf16), "r1": ((3, 3, 320, HALF), bf16), "t2": ((3, 320, HALF), bf16),
        "r2": ((3, 3, 80, HALF), bf16), "t3": ((3, 4, 32, HALF), bf16), "r3": ((3, 3, 32, HALF), bf16),
        "swap_out": ((3, 2, 16, HALF), f32), "rows_out": ((3, 16, D), f32), "rows_in": ((3, 16, D), f32),
        "gw": ((D, 256), f32), "gw_send": ((8, SHARD, 256), bf16), "gw_in": ((7, SHARD, 256), bf16),
        "gq_send": ((16, 16, 256), bf16), "gq_in": ((16, 16, 256), bf16),
        "ar_own": ((8, D), f32), "ar_one": ((16, 8, D), f32), "ar_mid": ((8, D), f32), "ar_two": ((8, 8, D), f32),
    }
    outs = {
        "layer_out": ((BLK, D), bf16), "input_grad": ((BLK, D), f32), "grad_mlp": ((3, 16, D), f32),
        "grad_qkv": ((16, 16, 256), bf16), "small_out": ((8, D), f32), "later_weights": ((3, D, D), bf16),
    }
    ins = (
        "lengths", "order", "tokens", "cot", "wqkv", "w_out", "w_up", "w_down", "w_query", "w_key", "w_value",
        "g_attn", "g_mlp", "q_scale", "b_up", "b_down",
    )

    def body(*refs):
        names = ins + tuple(outs) + tuple(shapes) + ("local_sems", "send_sems", "recv_sems")
        layer(**dict(zip(names, refs, strict=True)))

    row = lambda v: v.reshape(1, -1)
    out, in_grad, rows, qkv, small, _ = pl.pallas_call(
        body,
        out_shape=[jax.ShapeDtypeStruct(*s) for s in outs.values()],
        in_specs=[smem, smem] + [vmem] * 3 + [any_space] * 6 + [vmem] * 5,
        out_specs=[vmem] * (len(outs) - 1) + [any_space],
        scratch_shapes=[pltpu.VMEM(*s) for s in shapes.values()]
        + [pltpu.SemaphoreType.DMA((6,)), pltpu.SemaphoreType.DMA((N_SEM,)), pltpu.SemaphoreType.DMA((N_SEM,))],
        compiler_params=pltpu.CompilerParams(
            collective_id=0, has_side_effects=True, vmem_limit_bytes=62 << 20
        ),
    )(
        lengths, block_order, tokens[0], cotangent[0], wqkv, w_out, w_up, w_down, w_query, w_key, w_value,
        row(g_attn), row(g_mlp), row(q_scale), row(b_up), row(b_down),
    )
    heads = qkv[:, :10, :240].reshape(16, 10, 3, HEAD_DIM).astype(f32).transpose(2, 1, 0, 3).reshape(3, 10, D)
    grad_scale = small[4, :HEAD_DIM] * QUERY_CONST * jax.nn.sigmoid(q_scale)
    return (
        out[None], in_grad[None], heads[0], heads[1], heads[2], rows[0, :10], rows[1, :10], rows[2, :10],
        small[0], small[1], grad_scale, small[2], small[3],
    )


def solution(mesh):
    tokens, rows, whole = P("fsdp", "ctx", None), P("fsdp", None), P()
    owned = P(("ctx", "fsdp"), None)
    return jax.shard_map(
        on_device, mesh=mesh,
        in_specs=(tokens, tokens, rows, rows) + (rows,) * 6 + (whole,) * 5,
        out_specs=(tokens, tokens) + (owned,) * 6 + (whole,) * 5,
        check_vma=False,
    )
```

time: 1240 us -> 188 us (0.15)
  waiting for transfers between devices: 823 us -> 0 us
  matrix products: 240 us -> 0 us
  Pallas kernels: 0 us -> 165 us
  blocking collectives: 66.9 us -> 0 us
  local copies, waits for them, and re-layouts: 68.8 us -> 17.4 us
  other arithmetic: 22.6 us -> 2.88 us
  between operations: 14.2 us -> 0.7 us
    all_gather x8 -> x0, waiting for transfers between devices: 447 us -> none  [the longest x1 74 us: on_device(): lax.all_gather(w_key, 'fsdp', axis=0, tiled=True)]
    unnamed x14 -> x0, waiting for transfers between devices: 376 us -> none
    dot_general x130 -> x0, matrix products: 240 us -> none  [the longest x54 84.7 us: matmul_nt(): lax.dot_general(first_op, second_op, (((1,), (1,)), ((), ())), preferred_...]
    pallas_call x0 -> x1, Pallas kernels: none -> 165 us  [on_device(): pl.pallas_call(body, out_shape=[jax.ShapeDtypeStruct(*s) for s in outs.va...]
    psum x1 -> x0, blocking collectives: 66.9 us -> none  [on_device(): lax.psum((grad_gattn, grad_gmlp, grad_qscale, grad_bup, grad_bdown), ('ct...]
    unnamed x52 -> x2, local copies, waits for them, and re-layouts: 43.8 us -> 3.68 us
    all_gather x2 -> x0, local copies, waits for them, and re-layouts: 15.8 us -> none  [the longest x1 7.9 us: on_device(): lax.all_gather(key_rows, 'ctx', axis=0, tiled=True)]
  transfers between devices with their start and end apart: 11 -> 0, of which waited for: 11 -> 0; matrix products, arithmetic and copies ran while one was open for 13% -> 0% of each run, Pallas kernels for 0% -> 0%
where the time goes in v1:
time: 188 us; the launch traced here: 186 us
  Pallas kernels  165 us (88%)
  local copies, waits for them, and re-layouts  17.4 us (9%)
  other arithmetic  2.88 us (2%)
    pallas_call x1, Pallas kernels, on_device(): pl.pallas_call(body, out_shape=[jax.ShapeDtypeStruct(*s) for s in outs.va...  165 us
    reshape x4, local copies, waits for them, and re-layouts, on_device(): row = lambda v: v.reshape(1, -1)  5.17 us

profile of v1, /device:TPU:24, one launch (start us, length us, event | category | flops | bytes accessed | tf_op | source)
XLA Modules:
  0.0 186.2 jit_solution(11886772576172431427)
XLA Ops:
  0.7 0.1 pad.3.clone
  0.7 1.3 reshape.53.refs_11_
  2.0 1.3 reshape.54.refs_12_
  3.3 1.3 reshape.56.refs_14_
  4.6 1.3 reshape.57.refs_15_
  5.9 1.0 constant_dynamic-slice_fusion.2
  6.9 1.0 constant_dynamic-slice_fusion
  7.9 0.7 maximum_maximum_fusion.refs_4_
  8.6 165.3 %shard_map.246 = (bf16[128,1280]{1,0:T(8,128)(2,1)}, f32[128,1280]{1,0:T(8,128)}, f32[3,16,1280]{2,1,0:T(8,128)}, bf16[16,16,256]{2,1,0:T(8,128)(2,1)}, f32[8,12...) custom-call(s32[1,4]{1,0:T(1,128)} %refs_0_.1, s32[1,16]{1,0:T(1,128)} %refs_1_.1, bf16[128,1280]{1,0:T(8,128)(2,1)} %bitcast.18, ...), custom_call_target="tpu_custom_call" | custom-call | tf_op jit(solution)/shard_map/pallas_call | solution.py:590
  173.9 1.2 divide_multiply_fusion
  175.1 1.6 slice_reduce_fusion.3
  176.7 1.7 slice_bitcast_fusion
  178.4 0.9 slice_convert_fusion
  179.3 0.1 copy.32
  179.4 0.2 reshape.58
  179.6 0.7 slice_reduce_fusion
  180.3 0.7 squeeze.41
  181.1 0.7 squeeze.40
  181.8 0.7 squeeze.39
  182.5 1.7 copy.35
  184.2 2.0 %copy.36 = f32[1,128,1280]{2,1,0:T(8,128)} copy(f32[1,128,1280]{2,1,0:T(8,128)} %bitcast.17) | data formatting | bytes 1310720
  (1 shorter events, 0.0 us)

commit v2 on v1

--- a/solution.py
+++ b/solution.py
@@ -70,14 +70,14 @@
 
 
 def layer(
-    lengths, order, tokens, cot, wqkv, w_out, w_up, w_down, w_query, w_key, w_value,
+    lengths, order, tokens, cot, w_out, w_up, w_down, w_query, w_key, w_value,
     g_attn, g_mlp, q_scale, b_up, b_down,
     layer_out, input_grad, grad_mlp, grad_qkv, small_out,
     later_weights,
-    weights, gathered, wqkv_all, wqkv_t, raw_q, qkv_slot, qkv_pos, raw_pos, k_rows, v_rows, probs, out_pos,
+    weights, shards, gathered, wqkv_all, wqkv_t, raw_q, qkv_slot, qkv_pos, raw_pos, k_rows, v_rows, probs, out_pos,
     head_send, mixed_t, dout_t, dout_slot, dout_pos, dk_acc, dv_acc, grads_pos, grads_flat, grads_in,
     acts, up_in, up_all, t1, r1, t2, r2, t3, r3, swap_out, rows_out, rows_in,
-    gw, gw_send, gw_in, gq_send, gq_in, ar_own, ar_one, ar_mid, ar_two,
+    gw, gw_send, gw_in, gq_send, gq_in, ar_own, ar_half, ar_slots, ar_total,
     local_sems, send_sems, recv_sems,
 ):
     c, f = lax.axis_index("ctx"), lax.axis_index("fsdp")
@@ -107,8 +107,10 @@
 
     own_rows = ds(f * SHARD, SHARD, SHARD)
     loads = []
-    for j, ref in enumerate((w_out, w_up, w_down, w_query, w_key, w_value)):
-        load = pltpu.make_async_copy(ref, (weights, later_weights)[j // 3].at[j % 3, own_rows], local_sems.at[j])
+    for j, ref in enumerate((w_query, w_key, w_value, w_out, w_up, w_down)):
+        load = pltpu.make_async_copy(
+            ref, shards.at[j] if j < 3 else weights.at[j - 3, own_rows], local_sems.at[j]
+        )
         load.start()
         loads.append(load)
 
@@ -120,12 +122,24 @@
     for peer in peers:
         pl.semaphore_signal(barrier, inc=1, device_id=peer, device_id_type=MESH)
 
+    gain_one, gain_two = g_attn[...].reshape(1, D), g_mlp[...].reshape(1, D)
+    bias_up, bias_down = b_up[...].reshape(1, D), b_down[...].reshape(1, D)
     x_in = tokens[...].astype(f32)
     r_one = lax.rsqrt(jnp.mean(x_in * x_in, axis=1, keepdims=True) + EPS)
-    gathered[ds(c * BLK, BLK, BLK), :] = (x_in * r_one * g_attn[...]).astype(bf16)
-    wqkv_all[own_rows, :] = wqkv[...]
-    scale = QUERY_CONST * jnp.log(1.0 + jnp.exp(q_scale[...]))
+    gathered[ds(c * BLK, BLK, BLK), :] = (x_in * r_one * gain_one).astype(bf16)
+    scale = QUERY_CONST * jnp.log(1.0 + jnp.exp(q_scale[...].reshape(1, HEAD_DIM)))
     scale_col = jnp.broadcast_to(scale, (BLK, HEAD_DIM)).T[:, :1]
+
+    from_col = lax.broadcasted_iota(jnp.int32, (D, 256), 0) - c * HEAD_DIM
+    to_col = lax.broadcasted_iota(jnp.int32, (D, 256), 1)
+    own_cols = jnp.zeros((SHARD, 256), f32)
+    for j in range(3):
+        loads[j].wait()
+        pick = (from_col >= 0) & (from_col < HEAD_DIM) & (to_col == from_col + j * HEAD_DIM)
+        own_cols = own_cols + nn(shards[j], jnp.where(pick, 1.0, 0.0).astype(bf16))
+    wqkv_all[own_rows, :] = own_cols.astype(bf16)
+    keep = pltpu.make_async_copy(shards, later_weights.at[:, own_rows], local_sems.at[6])
+    keep.start()
 
     pl.semaphore_wait(barrier, len(peers))
 
@@ -137,61 +151,81 @@
 
     other = 1 - y_hi
     xl, xr, xo = (x + 3) % 4, (x + 1) % 4, (x + 2) % 4
-    own = piece(y_hi, x, core)
-    to_y = wire.send(own, own, away(dy=2))
-    to_xr = wire.send(own, own, away(dx=1))
-    to_xl = wire.send(own, own, away(dx=3))
-    to_core = wire.send(own, own, sibling)
-    cols = []
-    for k in range(1, 8):
-        cols.append(wire.send(wqkv_all.at[own_rows], wqkv_all.at[own_rows], (c, (f + k) % 8)))
+    def pass_chunk(yh, xa, part, device):
+        chunk = piece(yh, xa, core, part)
+        return wire.send(chunk, chunk, device)
+
+    left, right, across = away(dx=3), away(dx=1), away(dy=2)
+    to_y, to_xr, to_xl = {}, {}, {}
+    for one, other_one in ((0, 1), (1, 0)):
+        to_y[one] = pass_chunk(y_hi, x, one, across)
+        to_xr[one] = pass_chunk(y_hi, x, one, right)
+        to_xl[other_one] = pass_chunk(y_hi, x, other_one, left)
+    to_core = wire.send(piece(y_hi, x, core), piece(y_hi, x, core), sibling)
+
+    def columns_at(zz, lo):
+        return wqkv_all.at[ds((zz * 2 + lo) * SHARD, SHARD, SHARD)]
+
+    def columns_round_z(lo):
+        return [wire.send(columns_at(z, lo), columns_at(z, lo), away(dz=k)) for k in (1, 3, 2)]
+
+    pair = (c, f + 1 - 2 * y_lo)
+    cols_y = wire.send(columns_at(z, y_lo), columns_at(z, y_lo), pair)
+    cols_z = columns_round_z(y_lo)
 
     half_cols = ds(core * HALF, HALF, 128)
     across_y = (y + 1 + 2 * core) % 4
     from_y = (y + 3 + 2 * core) % 4
 
-    def rows_of(buffer, zz, lo, part=None):
-        start = (zz * 2 + lo) * SHARD
-        if part is None:
-            return buffer.at[:, ds(start, SHARD, SHARD), half_cols]
-        return buffer.at[:, ds(start + part * 80, 80, 80), half_cols]
+    def rows_of(view, zz, lo, first=0, count=SHARD):
+        buffer, at_first, number = view
+        return buffer.at[pl.ds(at_first, number), ds((zz * 2 + lo) * SHARD + first, count, 16), half_cols]
 
     zl, zr, zo = (z + 3) % 4, (z + 1) % 4, (z + 2) % 4
 
     class Gather:
-        def __init__(self, buffer, own):
-            self.buffer, self.own = buffer, own
+        def __init__(self, buffer, own, split):
+            self.buffer, self.own, self.split = buffer, own, split
+            self.first, self.count, self.left = (80 * (x % 2), 80, 48) if split else (0, SHARD, 80)
+            self.kept, self.over_x = [], []
+
+        def rows(self, zz, lo, part=None):
+            first, count = self.first, self.count
+            if part is not None:
+                first, count = (first, self.left) if part == 0 else (first + self.left, count - self.left)
+            return rows_of(self.buffer, zz, lo, first, count)
 
         def begin(self):
-            one = rows_of(self.buffer, z, y_lo)
-            for load in self.own:
-                load.wait()
-            self.y = wire.send(one, one, at(x, across_y, z, core))
-            self.r0 = wire.send(one, one, away(dz=1))
-            self.l0 = wire.send(one, one, away(dz=3))
-            self.kept = []
-
-        def give(self, ref):
+            own, one = self.own(self.first, self.count), self.rows(z, y_lo)
+            self.r0 = wire.send(own, one, away(dz=1))
+            self.l0 = wire.send(own, one, away(dz=3))
+
+        def begin_y(self):
+            self.y = wire.send(self.own(self.first, self.count), self.rows(z, y_lo), at(x, across_y, z, core))
+
+        def give(self, zz, lo):
+            ref = self.rows(zz, lo)
             self.kept.append((wire.send(ref, ref, sibling), ref))
+            if self.split:
+                self.over_x.append((wire.send(ref, ref, at((x + 1 + 2 * core) % 4, y, z, core)), zz, lo))
 
         def second(self):
-            two = rows_of(self.buffer, z, 1 - y_lo)
+            two = self.rows(z, 1 - y_lo)
             wire.receive(self.y, two, at(x, from_y, z, core))
             self.r1 = wire.send(two, two, away(dz=1))
             self.l1 = wire.send(two, two, away(dz=3))
-            self.give(two)
+            self.give(z, 1 - y_lo)
 
         def forward(self, lo, left, right):
-            a, b = rows_of(self.buffer, zl, lo), rows_of(self.buffer, zr, lo)
-            wire.receive(right, a, away(dz=3))
-            ah = rows_of(self.buffer, zl, lo, 0)
-            ka = wire.send(ah, ah, away(dz=1))
-            self.give(a)
-            wire.receive(left, b, away(dz=1))
-            bh = rows_of(self.buffer, zr, lo, 1)
-            kb = wire.send(bh, bh, away(dz=3))
-            self.give(b)
-            return ka, kb
+            wire.receive(right, self.rows(zl, lo), away(dz=3))
+            one = self.rows(zl, lo, 0)
+            to_right = wire.send(one, one, away(dz=1))
+            wire.receive(left, self.rows(zr, lo), away(dz=1))
+            two = self.rows(zr, lo, 1)
+            to_left = wire.send(two, two, away(dz=3))
+            self.give(zl, lo)
+            self.give(zr, lo)
+            return to_right, to_left
 
         def third(self):
             self.f0 = self.forward(y_lo, self.l0, self.r0)
@@ -200,22 +234,35 @@
             self.f1 = self.forward(1 - y_lo, self.l1, self.r1)
 
         def last(self, lo, pair):
-            wire.receive(pair[0], rows_of(self.buffer, zo, lo, 0), away(dz=3))
-            wire.receive(pair[1], rows_of(self.buffer, zo, lo, 1), away(dz=1))
-            self.give(rows_of(self.buffer, zo, lo))
+            wire.receive(pair[0], self.rows(zo, lo, 0), away(dz=3))
+            wire.receive(pair[1], self.rows(zo, lo, 1), away(dz=1))
+            self.give(zo, lo)
 
         def fifth(self):
             self.last(y_lo, self.f0)
 
         def sixth(self):
             self.last(1 - y_lo, self.f1)
+
+        def seventh(self):
+            for index, zz, lo in self.over_x:
+                ref = rows_of(self.buffer, zz, lo, 80 - self.first, 80)
+                wire.receive(index, ref, at((x + 3 + 2 * core) % 4, y, z, core))
+                self.kept.append((wire.send(ref, ref, sibling), ref))
 
         def finish(self):
             for index, ref in self.kept:
                 wire.receive(index, ref, sibling)
 
-    first_set, second_set = Gather(weights, loads[:3]), Gather(later_weights, loads[3:])
-    first_set.begin()
+    def early(j, split):
+        view = (weights, j, 1)
+        return Gather(view, lambda first, count: rows_of(view, z, y_lo, first, count), split)
+
+    out_rows, up_rows, down_rows = early(0, False), early(1, True), early(2, True)
+    second_set = Gather((later_weights, 0, 3), lambda first, count: shards.at[:, ds(first, count, 16), half_cols], True)
+    for load in loads[3:]:
+        load.wait()
+    out_rows.begin()
 
     def project(yh, xa):
         chip = yh * 4 + xa
@@ -226,47 +273,80 @@
             qkv_slot[2 * chip + i, :HEAD_DIM] = (one[:HEAD_DIM] * scale_col).astype(bf16)
             qkv_slot[2 * chip + i, HEAD_DIM:] = one[HEAD_DIM:240].astype(bf16)
 
-    for k, index in enumerate(cols):
-        src_f = (f + 7 - k) % 8
-        wire.receive(index, wqkv_all.at[ds(src_f * SHARD, SHARD, SHARD)], (c, src_f))
+    def take(indices, yh, xa, device, parts=(0, 1)):
+        for part in parts:
+            wire.receive(indices[part], piece(yh, xa, core, part), device)
+
+    def to_sibling(yh, xa):
+        return wire.send(piece(yh, xa, core), piece(yh, xa, core), sibling)
+
+    def both_cores(index, yh, xa):
+        wire.receive(index, piece(yh, xa, 1 - core), sibling)
+        project(yh, xa)
+
+    wire.receive(cols_y, columns_at(z, 1 - y_lo), pair)
+    cols_yz = columns_round_z(1 - y_lo)
+    down_rows.begin()
+    up_rows.begin()
+    ring, y_r, y_l = {}, {}, {}
+    take(to_xr, y_hi, xl, left, (0,))
+    ring[0] = pass_chunk(y_hi, xl, 0, right)
+    take(to_xl, y_hi, xr, right, (1,))
+    ring[1] = pass_chunk(y_hi, xr, 1, left)
+    take(to_y, other, x, across, (0,))
+    y_r[0] = pass_chunk(other, x, 0, right)
+    y_l[0] = pass_chunk(other, x, 0, left)
+    take(to_xr, y_hi, xl, left, (1,))
+    core_l = to_sibling(y_hi, xl)
+    take(to_xl, y_hi, xr, right, (0,))
+    core_r = to_sibling(y_hi, xr)
+    take(to_y, other, x, across, (1,))
+    y_r[1] = pass_chunk(other, x, 1, right)
+    y_l[1] = pass_chunk(other, x, 1, left)
+    core_y = to_sibling(other, x)
+    out_rows.begin_y()
+    down_rows.begin_y()
+    up_rows.begin_y()
+    for index, k in zip(cols_z, (1, 3, 2)):
+        wire.receive(index, columns_at((z + 4 - k) % 4, y_lo), away(dz=4 - k))
+    for index, k in zip(cols_yz, (1, 3, 2)):
+        wire.receive(index, columns_at((z + 4 - k) % 4, 1 - y_lo), away(dz=4 - k))
     wqkv_t[...] = flip(wqkv_all[...])
-
-    def pass_on(index, ref, device):
-        wire.receive(index, ref, device)
-        return wire.send(ref, ref, sibling)
-
-    wire.receive(to_core, piece(y_hi, x, 1 - core), sibling)
-    project(y_hi, x)
-    core_l = pass_on(to_xr, piece(y_hi, xl, core), away(dx=3))
-    ring_r = wire.send(piece(y_hi, xl, core, 0), piece(y_hi, xl, core, 0), away(dx=1))
-    core_r = pass_on(to_xl, piece(y_hi, xr, core), away(dx=1))
-    ring_l = wire.send(piece(y_hi, xr, core, 1), piece(y_hi, xr, core, 1), away(dx=3))
-    core_y = pass_on(to_y, piece(other, x, core), away(dy=2))
-    y_r = wire.send(piece(other, x, core), piece(other, x, core), away(dx=1))
-    y_l = wire.send(piece(other, x, core), piece(other, x, core), away(dx=3))
-    first_set.second()
-    wire.receive(core_l, piece(y_hi, xl, 1 - core), sibling)
-    project(y_hi, xl)
-    wire.receive(core_r, piece(y_hi, xr, 1 - core), sibling)
-    project(y_hi, xr)
-    wire.receive(core_y, piece(other, x, 1 - core), sibling)
-    project(other, x)
-    wire.receive(ring_r, piece(y_hi, xo, core, 0), away(dx=3))
-    wire.receive(ring_l, piece(y_hi, xo, core, 1), away(dx=1))
-    far = wire.send(piece(y_hi, xo, core), piece(y_hi, xo, core), away(dy=2))
-    core_o = wire.send(piece(y_hi, xo, core), piece(y_hi, xo, core), sibling)
-    core_yl = pass_on(y_r, piece(other, xl, core), away(dx=3))
-    core_yr = pass_on(y_l, piece(other, xr, core), away(dx=1))
-    first_set.third()
-    wire.receive(core_o, piece(y_hi, xo, 1 - core), sibling)
-    project(y_hi, xo)
-    wire.receive(core_yl, piece(other, xl, 1 - core), sibling)
-    project(other, xl)
-    wire.receive(core_yr, piece(other, xr, 1 - core), sibling)
-    project(other, xr)
-    core_f = pass_on(far, piece(other, xo, core), away(dy=2))
-    wire.receive(core_f, piece(other, xo, 1 - core), sibling)
-    project(other, xo)
+    far = {}
+    wire.receive(ring[0], piece(y_hi, xo, core, 0), left)
+    far[0] = pass_chunk(y_hi, xo, 0, across)
+    wire.receive(ring[1], piece(y_hi, xo, core, 1), right)
+    far[1] = pass_chunk(y_hi, xo, 1, across)
+    core_o = to_sibling(y_hi, xo)
+    both_cores(to_core, y_hi, x)
+    both_cores(core_l, y_hi, xl)
+    out_rows.second()
+    out_rows.third()
+    both_cores(core_r, y_hi, xr)
+    both_cores(core_y, other, x)
+    both_cores(core_o, y_hi, xo)
+    take(y_r, other, xl, left)
+    core_yl = to_sibling(other, xl)
+    take(y_l, other, xr, right)
+    core_yr = to_sibling(other, xr)
+    down_rows.second()
+    up_rows.second()
+    both_cores(core_yl, other, xl)
+    both_cores(core_yr, other, xr)
+    take(far, other, xo, across)
+    core_f = to_sibling(other, xo)
+    out_rows.fourth()
+    both_cores(core_f, other, xo)
+
+    waiting = [
+        down_rows.third, up_rows.third, second_set.begin_y, second_set.begin, out_rows.fifth, down_rows.fourth,
+        up_rows.fourth, out_rows.sixth, down_rows.fifth, up_rows.fifth, down_rows.sixth, up_rows.sixth,
+    ]
+
+    def move_on(number):
+        for _ in range(number):
+            if waiting:
+                waiting.pop(0)()
 
     slot_of = []
     for p in range(NBLK):
@@ -308,6 +388,7 @@
         out = nn(qkv_pos[2 * HEAD_DIM:, low:high], part).astype(bf16)
         out_pos[2 * t] = out[:, :BLK]
         out_pos[2 * t + 1] = out[:, BLK:]
+        move_on(1)
 
     for b in range(NBLK):
         head_send[b] = out_pos[order[0, b]]
@@ -323,12 +404,11 @@
     head_rows = ds(c * HEAD_DIM, HEAD_DIM, HEAD_DIM)
     mixing = exchange(lambda b: head_send.at[b], mixed_t.at[head_rows])
     mixed_t[head_rows, :] = head_send[c]
-    first_set.fourth()
-    first_set.fifth()
-    first_set.sixth()
-    first_set.finish()
-    wire.set_one = len(wire.sent)
-    second_set.begin()
+    move_on(len(waiting))
+    down_rows.seventh()
+    up_rows.seventh()
+    second_set.second()
+    down_rows.finish()
 
     cot_f = cot[...].astype(f32)
 
@@ -341,17 +421,20 @@
     grad_active = spread_back(cot[...], 2)
     arrive(mixing, lambda src: mixed_t.at[ds(src * HEAD_DIM, HEAD_DIM, HEAD_DIM)])
 
+    out_rows.finish()
     mixed = flip(mixed_t[...])
     after = x_in + spread(mixed, 0)
     r_two = lax.rsqrt(jnp.mean(after * after, axis=1, keepdims=True) + EPS)
     n_two = after * r_two
-    normed_two = (n_two * g_mlp[...]).astype(bf16)
-    hidden = spread(normed_two, 1) + b_up[...]
+    normed_two = (n_two * gain_two).astype(bf16)
+    up_rows.finish()
+    wire.set_one = len(wire.sent)
+    hidden = spread(normed_two, 1) + bias_up
     gate = jax.nn.sigmoid(hidden)
     active = (hidden * gate).astype(bf16)
     grad_hidden = (grad_active * gate * (1.0 + hidden * (1.0 - gate))).astype(bf16)
     back_two = spread_back(grad_hidden, 1)
-    scaled = back_two * g_mlp[...]
+    scaled = back_two * gain_two
     grad_after = cot_f + r_two * (scaled - n_two * jnp.mean(scaled * n_two, axis=1, keepdims=True))
     grad_branch = grad_after.astype(bf16)
     dout_t[...] = flip(spread_back(grad_branch, 0).astype(bf16))
@@ -370,14 +453,14 @@
     give_up = wire.send(up_in.at[:, :, other_half], up_all.at[:, my_lanes], sibling)
     for w in range(3):
         up_all[w, my_lanes, :] = up_in[w, :, half_cols]
-    layer_out[...] = (after + spread(active, 2) + b_down[...]).astype(bf16)
+    layer_out[...] = (after + spread(active, 2) + bias_down).astype(bf16)
     input_grad[...] = grad_after
     ar_own[...] = jnp.zeros_like(ar_own)
     ar_own[1:2, :] = jnp.sum(back_two * n_two, axis=0, keepdims=True)
     ar_own[2:3, :] = jnp.sum(grad_hidden.astype(f32), axis=0, keepdims=True)
     ar_own[3:4, :] = jnp.sum(cot_f, axis=0, keepdims=True)
 
-    second_set.second()
+    second_set.third()
     sib_lanes = ds((1 - core) * BLK, BLK, BLK)
     wire.receive(give_acts, acts.at[:, :, sib_lanes], sibling)
     wire.receive(give_up, up_all.at[:, sib_lanes], sibling)
@@ -420,6 +503,7 @@
         rows_out[w, :, half_cols] = swap_out[w, core]
         return wire.send(swap_out.at[w, 1 - core], rows_out.at[w, :, half_cols], sibling)
 
+    second_set.fourth()
     arrive(douts, lambda src: dout_slot.at[src])
 
     for p in range(NBLK):
@@ -441,6 +525,8 @@
         dq = (dq * scale_col).astype(bf16)
         grads_pos[2 * t, :HEAD_DIM] = dq[:, :BLK]
         grads_pos[2 * t + 1, :HEAD_DIM] = dq[:, BLK:]
+        if t in (3, 6):
+            (second_set.fifth, second_set.sixth)[t // 4]()
         dk_acc[:, low:high] += nt(qkv_pos[:HEAD_DIM, tile], d_scores)
         dv_acc[:, low:high] += nt(d_out, part)
 
@@ -455,28 +541,58 @@
     sent_grads = exchange(lambda b: qkv_slot.at[b], grads_in.at[c])
     grads_in[c] = qkv_slot[c]
 
-    second_set.third()
-    second_set.fourth()
-
     for n in range(0, D, 256):
         grad_t = nn(grads_flat[...], gathered[:, n:n + 256])
+        by_gain = jnp.sum(wqkv_t[:240, n:n + 256].astype(f32) * grad_t, axis=0, keepdims=True)
+        ar_own[0:1, n:n + 256] = by_gain / gain_one[:, n:n + 256]
         gw[n:n + 256, :] = jnp.concatenate([grad_t, jnp.zeros((16, 256), f32)], axis=0).T
     for fs in range(8):
         picked = [gw[cs * 80 + fs * 10:cs * 80 + fs * 10 + 10, :] for cs in range(16)]
         gw_send[fs] = jnp.concatenate(picked, axis=0).astype(bf16)
+    ar_own[4:5, :HEAD_DIM] = jnp.broadcast_to(scale_terms, (HEAD_DIM, BLK)).T[:1]
+    half_sums = wire.send(ar_own.at[:, other_half], ar_half, sibling)
     shares = [wire.send(gw_send.at[(f + k) % 8], gw_in.at[k - 1], (c, (f + k) % 8)) for k in range(1, 8)]
 
-    for w in (2, 1, 0):
-        second_stage(w)
-    second_set.fifth()
-    second_set.sixth()
+    def spread_sums(i, axis, value):
+        me = here[axis]
+        ar_slots[i, me] = value
+        return [wire.send(ar_slots.at[i, me], ar_slots.at[i, me], away(**{"d" + axis: k})) for k in range(1, 4)]
+
+    def collect_sums(i, axis, indices):
+        for k, index in enumerate(indices):
+            wire.receive(index, ar_slots.at[i, (here[axis] + 3 - k) % 4], away(**{"d" + axis: 3 - k}))
+        return ar_slots[i, 0] + ar_slots[i, 1] + ar_slots[i, 2] + ar_slots[i, 3]
+
+    wire.receive(half_sums, ar_half, sibling)
+    sums = spread_sums(0, "x", ar_own[:, half_cols] + ar_half[...])
+    second_set.seventh()
+    second_stage(2)
+    sums = spread_sums(1, "y", collect_sums(0, "x", sums))
+    second_stage(1)
+    second_stage(0)
+    sums = spread_sums(2, "z", collect_sums(1, "y", sums))
+
+    for k, index in enumerate(shares):
+        src_f = (f + 7 - k) % 8
+        wire.receive(index, gw_in.at[k], (c, src_f))
+    both = gw_send[f].astype(f32)
+    for k in range(7):
+        both = both + gw_in[k].astype(f32)
+    for cs in range(16):
+        gq_send[cs] = jnp.concatenate([both[10 * cs:10 * cs + 10], jnp.zeros((6, 256), f32)], axis=0).astype(bf16)
+    gq_in[c] = gq_send[c]
+    heads = exchange(lambda b: gq_send.at[b], gq_in.at[c])
+    third_stage(2)
+    third_stage(1)
+    third_stage(0)
+    ar_total[:, half_cols] = collect_sums(2, "z", sums)
+    half_sums = wire.send(ar_total.at[:, half_cols], ar_total.at[:, half_cols], sibling)
+
     second_set.finish()
-    for w in (2, 1, 0):
-        third_stage(w)
-
     for copy in wire.sent[:wire.set_one]:
         copy.wait_send()
     wire.sent = wire.sent[wire.set_one:]
+    keep.wait()
     loads = []
     for j in range(3):
         load = pltpu.make_async_copy(later_weights.at[j], weights.at[j], local_sems.at[j])
@@ -490,26 +606,11 @@
         joined = jnp.concatenate([grads_in[h, rows] for h in range(HEADS)], axis=0)
         grad_normed = grad_normed + spread_back(flip(joined), j)
     n_one = x_in * r_one
-    scaled = grad_normed * g_attn[...]
+    scaled = grad_normed * gain_one
     through = r_one * (scaled - n_one * jnp.mean(scaled * n_one, axis=1, keepdims=True))
     input_grad[...] = input_grad[...] + through
-    ar_own[0:1, :] = jnp.sum(grad_normed * n_one, axis=0, keepdims=True)
-    ar_own[4:5, :HEAD_DIM] = jnp.broadcast_to(scale_terms, (HEAD_DIM, BLK)).T[:1]
-    ar_one[c] = ar_own[...]
-    sums = exchange(lambda b: ar_own, ar_one.at[c])
 
     swaps = [(w, fourth_stage(w)) for w in (2, 1, 0)]
-    for k, index in enumerate(shares):
-        src_f = (f + 7 - k) % 8
-        wire.receive(index, gw_in.at[k], (c, src_f))
-    both = gw_send[f].astype(f32)
-    for k in range(7):
-        both = both + gw_in[k].astype(f32)
-    for cs in range(16):
-        gq_send[cs] = jnp.concatenate([both[10 * cs:10 * cs + 10], jnp.zeros((6, 256), f32)], axis=0).astype(bf16)
-    gq_in[c] = gq_send[c]
-    heads = exchange(lambda b: gq_send.at[b], gq_in.at[c])
-
     finals = []
     for w, index in swaps:
         wire.receive(index, rows_out.at[w, :, other_half], sibling)
@@ -523,21 +624,8 @@
         pl.when(stays)(within.start)
         finals.append((w, index, copy, stays))
 
-    arrive(sums, lambda src: ar_one.at[src])
-    total_small = ar_one[0]
-    for k in range(1, 16):
-        total_small = total_small + ar_one[k]
-    ar_mid[...] = total_small
-    ar_two[f] = total_small
-    sums = [wire.send(ar_mid, ar_two.at[f], (c, (f + k) % 8)) for k in range(1, 8)]
-    for k, index in enumerate(sums):
-        src_f = (f + 7 - k) % 8
-        wire.receive(index, ar_two.at[src_f], (c, src_f))
-    total_small = ar_two[0]
-    for k in range(1, 8):
-        total_small = total_small + ar_two[k]
-    small_out[...] = total_small
-
+    wire.receive(half_sums, ar_total.at[:, other_half], sibling)
+    small_out[...] = ar_total[...]
     arrive(heads, lambda src: gq_in.at[src])
     grad_qkv[...] = gq_in[...]
     for w, index, copy, stays in finals:
@@ -548,16 +636,44 @@
     assert wire.used <= N_SEM
 
 
+def outputs(
+    out, in_grad, rows, qkv, small, q_scale,
+    layer_out, input_grad, g_query, g_key, g_value, g_out, g_up, g_down, g_gain_one, g_gain_two, g_scale, g_bias_up, g_bias_down,
+    rows_here, qkv_here, small_here, sems,
+):
+    places = (layer_out.at[0], input_grad.at[0], rows_here, qkv_here, small_here)
+    copies = [
+        pltpu.make_async_copy(src, dst, sems.at[i]) for i, (src, dst) in enumerate(zip((out, in_grad, rows, qkv, small), places))
+    ]
+    for copy in copies:
+        copy.start()
+    for copy in copies:
+        copy.wait()
+    rows, qkv, small = rows_here, qkv_here, small_here
+    for j, ref in enumerate((g_query, g_key, g_value)):
+        tiles = [jnp.zeros((16, BLK), f32) for _ in range(11)]
+        for h in range(HEADS):
+            tile, start = divmod(h * HEAD_DIM, BLK)
+            moved = pltpu.roll(qkv[h].astype(f32), (start - j * HEAD_DIM) % 256, 1)
+            lane = lax.broadcasted_iota(jnp.int32, (16, 256), 1)
+            moved = jnp.where((lane >= start) & (lane < start + HEAD_DIM), moved, 0.0)
+            tiles[tile] = tiles[tile] + moved[:, :BLK]
+            tiles[tile + 1] = tiles[tile + 1] + moved[:, BLK:]
+        ref[...] = jnp.concatenate(tiles[:10], axis=1)[:10]
+    for w, ref in enumerate((g_out, g_up, g_down)):
+        ref[...] = rows[w, :10, :]
+    for i, ref in ((0, g_gain_one), (1, g_gain_two), (2, g_bias_up), (3, g_bias_down)):
+        ref[...] = small[i, :]
+    g_scale[...] = small[4, :HEAD_DIM] * QUERY_CONST * jax.nn.sigmoid(q_scale[...])
+
+
 def on_device(
     tokens, cotangent, lengths, block_order, w_query, w_key, w_value, w_out, w_up, w_down,
     g_attn, g_mlp, q_scale, b_up, b_down,
 ):
-    first = lax.axis_index("ctx") * HEAD_DIM
-    columns = [lax.dynamic_slice(w, (0, first), (SHARD, HEAD_DIM)) for w in (w_query, w_key, w_value)]
-    wqkv = jnp.concatenate(columns + [jnp.zeros((SHARD, 16), bf16)], axis=1)
     vmem, smem, any_space = (pl.BlockSpec(memory_space=s) for s in (pltpu.VMEM, pltpu.SMEM, pl.ANY))
     shapes = {
-        "weights": ((3, D, D), bf16), "gathered": ((GROUP, D), bf16), "wqkv_all": ((D, 256), bf16),
+        "weights": ((3, D, D), bf16), "shards": ((3, SHARD, D), bf16), "gathered": ((GROUP, D), bf16), "wqkv_all": ((D, 256), bf16),
         "wqkv_t": ((256, D), bf16), "raw_q": ((NBLK, HEAD_DIM, BLK), f32), "qkv_slot": ((NBLK, 240, BLK), bf16),
         "qkv_pos": ((240, GROUP), bf16), "raw_pos": ((HEAD_DIM, GROUP), f32), "k_rows": ((GROUP, HEAD_DIM), bf16),
         "v_rows": ((GROUP, HEAD_DIM), bf16), "probs": ((7680, TILE), bf16), "out_pos": ((NBLK, HEAD_DIM, BLK), bf16),
@@ -571,14 +687,15 @@
         "swap_out": ((3, 2, 16, HALF), f32), "rows_out": ((3, 16, D), f32), "rows_in": ((3, 16, D), f32),
         "gw": ((D, 256), f32), "gw_send": ((8, SHARD, 256), bf16), "gw_in": ((7, SHARD, 256), bf16),
         "gq_send": ((16, 16, 256), bf16), "gq_in": ((16, 16, 256), bf16),
-        "ar_own": ((8, D), f32), "ar_one": ((16, 8, D), f32), "ar_mid": ((8, D), f32), "ar_two": ((8, 8, D), f32),
+        "ar_own": ((8, D), f32), "ar_half": ((8, HALF), f32), "ar_slots": ((3, 4, 8, HALF), f32),
+        "ar_total": ((8, D), f32),
     }
     outs = {
         "layer_out": ((BLK, D), bf16), "input_grad": ((BLK, D), f32), "grad_mlp": ((3, 16, D), f32),
         "grad_qkv": ((16, 16, 256), bf16), "small_out": ((8, D), f32), "later_weights": ((3, D, D), bf16),
     }
     ins = (
-        "lengths", "order", "tokens", "cot", "wqkv", "w_out", "w_up", "w_down", "w_query", "w_key", "w_value",
+        "lengths", "order", "tokens", "cot", "w_out", "w_up", "w_down", "w_query", "w_key", "w_value",
         "g_attn", "g_mlp", "q_scale", "b_up", "b_down",
     )
 
@@ -586,27 +703,36 @@
         names = ins + tuple(outs) + tuple(shapes) + ("local_sems", "send_sems", "recv_sems")
         layer(**dict(zip(names, refs, strict=True)))
 
-    row = lambda v: v.reshape(1, -1)
     out, in_grad, rows, qkv, small, _ = pl.pallas_call(
         body,
         out_shape=[jax.ShapeDtypeStruct(*s) for s in outs.values()],
-        in_specs=[smem, smem] + [vmem] * 3 + [any_space] * 6 + [vmem] * 5,
+        in_specs=[smem, smem] + [vmem] * 2 + [any_space] * 6 + [vmem] * 5,
         out_specs=[vmem] * (len(outs) - 1) + [any_space],
         scratch_shapes=[pltpu.VMEM(*s) for s in shapes.values()]
-        + [pltpu.SemaphoreType.DMA((6,)), pltpu.SemaphoreType.DMA((N_SEM,)), pltpu.SemaphoreType.DMA((N_SEM,))],
+        + [pltpu.SemaphoreType.DMA((7,)), pltpu.SemaphoreType.DMA((N_SEM,)), pltpu.SemaphoreType.DMA((N_SEM,))],
         compiler_params=pltpu.CompilerParams(
             collective_id=0, has_side_effects=True, vmem_limit_bytes=62 << 20
         ),
     )(
-        lengths, block_order, tokens[0], cotangent[0], wqkv, w_out, w_up, w_down, w_query, w_key, w_value,
-        row(g_attn), row(g_mlp), row(q_scale), row(b_up), row(b_down),
+        lengths, block_order, tokens[0], cotangent[0], w_out, w_up, w_down, w_query, w_key, w_value,
+        g_attn, g_mlp, q_scale, b_up, b_down,
     )
-    heads = qkv[:, :10, :240].reshape(16, 10, 3, HEAD_DIM).astype(f32).transpose(2, 1, 0, 3).reshape(3, 10, D)
-    grad_scale = small[4, :HEAD_DIM] * QUERY_CONST * jax.nn.sigmoid(q_scale)
-    return (
-        out[None], in_grad[None], heads[0], heads[1], heads[2], rows[0, :10], rows[1, :10], rows[2, :10],
-        small[0], small[1], grad_scale, small[2], small[3],
-    )
+    row = jax.ShapeDtypeStruct((10, D), f32)
+    vector = jax.ShapeDtypeStruct((D,), f32)
+    return pl.pallas_call(
+        outputs,
+        out_shape=[
+            jax.ShapeDtypeStruct((1, BLK, D), bf16), jax.ShapeDtypeStruct((1, BLK, D), f32), *[row] * 6,
+            vector, vector, jax.ShapeDtypeStruct((HEAD_DIM,), f32), vector, vector,
+        ],
+        in_specs=[any_space] * 5 + [vmem],
+        out_specs=[vmem] * 13,
+        scratch_shapes=[
+            pltpu.VMEM((3, 16, D), f32), pltpu.VMEM((16, 16, 256), bf16), pltpu.VMEM((8, D), f32),
+            pltpu.SemaphoreType.DMA((5,)),
+        ],
+        compiler_params=pltpu.CompilerParams(vmem_limit_bytes=62 << 20),
+    )(out, in_grad, rows, qkv, small, q_scale)
 
 
 def solution(mesh):

time: 188 us -> 154 us (0.82)
  local copies, waits for them, and re-layouts: 17.4 us -> 0 us
  Pallas kernels: 165 us -> 153 us
  other arithmetic: 2.88 us -> 0 us
    pallas_call x1, Pallas kernels: 165 us -> 150 us  [on_device(): pl.pallas_call(body, out_shape=[jax.ShapeDtypeStruct(*s) for s in outs.va...]
    reshape x4 -> x0, local copies, waits for them, and re-layouts: 5.17 us -> none  [on_device(): row = lambda v: v.reshape(1, -1)]
    squeeze x4 -> x0, local copies, waits for them, and re-layouts: 3.87 us -> none  [the longest x1 1.66 us: on_device(): rows[2, :10]]
    unnamed x2 -> x0, local copies, waits for them, and re-layouts: 3.68 us -> none
    pallas_call x0 -> x1, Pallas kernels: none -> 3.11 us  [on_device(): pl.pallas_call(outputs, out_shape=[jax.ShapeDtypeStruct((1, BLK, D), bf16...]
    slice x2 -> x0, local copies, waits for them, and re-layouts: 2.29 us -> none  [the longest x1 1.61 us: on_device(): small[3]]
    dynamic_slice x2 -> x0, local copies, waits for them, and re-layouts: 1.99 us -> none  [on_device(): lax.dynamic_slice(w, (0, first), (SHARD, HEAD_DIM))]
where the time goes in v2:
time: 154 us
  Pallas kernels  153 us (99%)
    pallas_call x1, Pallas kernels, on_device(): pl.pallas_call(body, out_shape=[jax.ShapeDtypeStruct(*s) for s in outs.va...  150 us
    pallas_call x1, Pallas kernels, on_device(): pl.pallas_call(outputs, out_shape=[jax.ShapeDtypeStruct((1, BLK, D), bf16...  3.11 us

profile of v2, /device:TPU:24, one launch (start us, length us, event | category | flops | bytes accessed | tf_op | source)
XLA Modules:
  0.0 153.9 jit_solution(14071031447551653195)
XLA Ops:
  0.7 150.0 %shard_map.246 = (bf16[128,1280]{1,0:T(8,128)(2,1)}, f32[128,1280]{1,0:T(8,128)}, f32[3,16,1280]{2,1,0:T(8,128)}, bf16[16,16,256]{2,1,0:T(8,128)(2,1)}, f32[8,12...) custom-call(s32[1,4]{1,0:T(1,128)} %refs_0_.1, s32[1,16]{1,0:T(1,128)} %refs_1_.1, bf16[128,1280]{1,0:T(8,128)(2,1)} %bitcast.2, ...), custom_call_target="tpu_custom_call" | custom-call | tf_op jit(solution)/shard_map/pallas_call | solution.py:706
  150.6 3.1 %shard_map.247 = (bf16[1,128,1280]{2,1,0:T(8,128)(2,1)}, f32[1,128,1280]{2,1,0:T(8,128)}, f32[10,1280]{1,0:T(8,128)}, f32[10,1280]{1,0:T(8,128)}, f32[10,1280]{1...) custom-call(bf16[128,1280]{1,0:T(8,128)(2,1)} %get-tuple-element.18., ...), custom_call_target="tpu_custom_call" | custom-call | tf_op jit(solution)/shard_map/pallas_call | solution.py:722

commit v3 on v2

--- a/solution.py
+++ b/solution.py
@@ -21,7 +21,8 @@
 EPS = 1e-06
 QUERY_CONST = 1.442695 / math.sqrt(HEAD_DIM)
 MASKED = -1e30
-N_SEM = 256
+N_SEM = 288
+ORDERS = (("yxz", "yxz"), ("xzy", "xzy"), ("zyx", "zyx"))
 MESH = pl.DeviceIdType.MESH
 bf16, f32 = jnp.bfloat16, jnp.float32
 
@@ -76,7 +77,7 @@
     later_weights,
     weights, shards, gathered, wqkv_all, wqkv_t, raw_q, qkv_slot, qkv_pos, raw_pos, k_rows, v_rows, probs, out_pos,
     head_send, mixed_t, dout_t, dout_slot, dout_pos, dk_acc, dv_acc, grads_pos, grads_flat, grads_in,
-    acts, up_in, up_all, t1, r1, t2, r2, t3, r3, swap_out, rows_out, rows_in,
+    acts, up_in, up_all, t1, r1, t2, r2, t3, r3, rows_out, rows_in,
     gw, gw_send, gw_in, gq_send, gq_in, ar_own, ar_half, ar_slots, ar_total,
     local_sems, send_sems, recv_sems,
 ):
@@ -94,16 +95,24 @@
     sibling = (c + 1 - 2 * core, f)
     wire = Wire(send_sems, recv_sems)
 
-    axes = {0: "xzy", 1: "yxz", 2: "zyx"}
     here = {"x": x, "y": y, "z": z}
 
-    def final_target(w):
-        a, b, last = (here[n] for n in axes[w])
-        return (4 * a + b, 2 * last + core)
-
-    def final_source(w):
-        found = dict(zip(axes[w], (c // 4, c % 4, f // 2)))
-        return at(found["x"], found["y"], found["z"], f % 2)
+    def by_core(w, of):
+        first, second = (of(text) for text in ORDERS[w])
+        return first + core * (second - first)
+
+    def along(w, stage, k):
+        return away(**{"d" + axis: k * by_core(w, lambda text: int(text[stage] == axis)) for axis in "xyz"})
+
+    def place(w, stage):
+        return by_core(w, lambda text: here[text[stage]])
+
+    def final_target(w, i):
+        return (4 * place(w, 0) + place(w, 1), 2 * place(w, 2) + i)
+
+    def final_source(w, core_at):
+        found = dict(zip(ORDERS[w][core_at], (c // 4, c % 4, f // 2)))
+        return at(found["x"], found["y"], found["z"], core_at)
 
     own_rows = ds(f * SHARD, SHARD, SHARD)
     loads = []
@@ -118,7 +127,7 @@
     peers = [((c + k) % 16, f) for k in range(1, 16)] + [(c, (f + k) % 8) for k in range(1, 8)]
     peers.append(at(x, 3 - y, z, core))
     for w in range(3):
-        peers += [final_target(w), final_source(w)]
+        peers += [final_target(w, i) for i in range(2)] + [final_source(w, i) for i in range(2)]
     for peer in peers:
         pl.semaphore_signal(barrier, inc=1, device_id=peer, device_id_type=MESH)
 
@@ -157,20 +166,20 @@
 
     left, right, across = away(dx=3), away(dx=1), away(dy=2)
     to_y, to_xr, to_xl = {}, {}, {}
+    def columns_at(zz, lo):
+        return wqkv_all.at[ds((zz * 2 + lo) * SHARD, SHARD, SHARD)]
+
+    def columns_round_z(lo):
+        return [wire.send(columns_at(z, lo), columns_at(z, lo), away(dz=k)) for k in (1, 3, 2)]
+
+    pair = (c, f + 1 - 2 * y_lo)
     for one, other_one in ((0, 1), (1, 0)):
         to_y[one] = pass_chunk(y_hi, x, one, across)
         to_xr[one] = pass_chunk(y_hi, x, one, right)
         to_xl[other_one] = pass_chunk(y_hi, x, other_one, left)
+        if one == 0:
+            cols_y = wire.send(columns_at(z, y_lo), columns_at(z, y_lo), pair)
     to_core = wire.send(piece(y_hi, x, core), piece(y_hi, x, core), sibling)
-
-    def columns_at(zz, lo):
-        return wqkv_all.at[ds((zz * 2 + lo) * SHARD, SHARD, SHARD)]
-
-    def columns_round_z(lo):
-        return [wire.send(columns_at(z, lo), columns_at(z, lo), away(dz=k)) for k in (1, 3, 2)]
-
-    pair = (c, f + 1 - 2 * y_lo)
-    cols_y = wire.send(columns_at(z, y_lo), columns_at(z, y_lo), pair)
     cols_z = columns_round_z(y_lo)
 
     half_cols = ds(core * HALF, HALF, 128)
@@ -318,19 +327,21 @@
     wire.receive(ring[1], piece(y_hi, xo, core, 1), right)
     far[1] = pass_chunk(y_hi, xo, 1, across)
     core_o = to_sibling(y_hi, xo)
+    out_rows.third()
     both_cores(to_core, y_hi, x)
     both_cores(core_l, y_hi, xl)
+    both_cores(core_r, y_hi, xr)
     out_rows.second()
-    out_rows.third()
-    both_cores(core_r, y_hi, xr)
     both_cores(core_y, other, x)
-    both_cores(core_o, y_hi, xo)
     take(y_r, other, xl, left)
     core_yl = to_sibling(other, xl)
     take(y_l, other, xr, right)
     core_yr = to_sibling(other, xr)
     down_rows.second()
     up_rows.second()
+    both_cores(core_o, y_hi, xo)
+    down_rows.third()
+    up_rows.third()
     both_cores(core_yl, other, xl)
     both_cores(core_yr, other, xr)
     take(far, other, xo, across)
@@ -339,8 +350,8 @@
     both_cores(core_f, other, xo)
 
     waiting = [
-        down_rows.third, up_rows.third, second_set.begin_y, second_set.begin, out_rows.fifth, down_rows.fourth,
-        up_rows.fourth, out_rows.sixth, down_rows.fifth, up_rows.fifth, down_rows.sixth, up_rows.sixth,
+        down_rows.fourth, up_rows.fourth, out_rows.fifth, second_set.begin_y, second_set.begin,
+        down_rows.fifth, up_rows.fifth, out_rows.sixth, down_rows.sixth, up_rows.sixth,
     ]
 
     def move_on(number):
@@ -405,10 +416,7 @@
     mixing = exchange(lambda b: head_send.at[b], mixed_t.at[head_rows])
     mixed_t[head_rows, :] = head_send[c]
     move_on(len(waiting))
-    down_rows.seventh()
-    up_rows.seventh()
     second_set.second()
-    down_rows.finish()
 
     cot_f = cot[...].astype(f32)
 
@@ -418,21 +426,39 @@
     def spread_back(a, w):
         return jnp.concatenate([nt(a, weights[w, n:n + 256, :]) for n in range(0, D, 256)], axis=1)
 
-    grad_active = spread_back(cot[...], 2)
+    out_rows.finish()
     arrive(mixing, lambda src: mixed_t.at[ds(src * HEAD_DIM, HEAD_DIM, HEAD_DIM)])
 
-    out_rows.finish()
+    my_lanes, sib_lanes = ds(core * BLK, BLK, BLK), ds((1 - core) * BLK, BLK, BLK)
+    other_half = ds((1 - core) * HALF, HALF, 128)
+
+    def share(w, rows_t, up):
+        acts[w, :, my_lanes] = rows_t
+        up_in[w] = up
+        indices = (
+            wire.send(acts.at[w, :, my_lanes], acts.at[w, :, my_lanes], sibling),
+            wire.send(up_in.at[w, :, other_half], up_all.at[w, my_lanes], sibling),
+        )
+        up_all[w, my_lanes, :] = up_in[w, :, half_cols]
+        return indices
+
     mixed = flip(mixed_t[...])
     after = x_in + spread(mixed, 0)
     r_two = lax.rsqrt(jnp.mean(after * after, axis=1, keepdims=True) + EPS)
     n_two = after * r_two
     normed_two = (n_two * gain_two).astype(bf16)
+    up_rows.seventh()
+    down_rows.seventh()
     up_rows.finish()
-    wire.set_one = len(wire.sent)
     hidden = spread(normed_two, 1) + bias_up
     gate = jax.nn.sigmoid(hidden)
     active = (hidden * gate).astype(bf16)
+    shared = {2: share(2, flip(active), cot[...])}
+    down_rows.finish()
+    wire.set_one = len(wire.sent)
+    grad_active = spread_back(cot[...], 2)
     grad_hidden = (grad_active * gate * (1.0 + hidden * (1.0 - gate))).astype(bf16)
+    shared[1] = share(1, flip(normed_two), grad_hidden)
     back_two = spread_back(grad_hidden, 1)
     scaled = back_two * gain_two
     grad_after = cot_f + r_two * (scaled - n_two * jnp.mean(scaled * n_two, axis=1, keepdims=True))
@@ -440,68 +466,63 @@
     dout_t[...] = flip(spread_back(grad_branch, 0).astype(bf16))
     douts = exchange(lambda b: dout_t.at[ds(b * HEAD_DIM, HEAD_DIM, HEAD_DIM)], dout_slot.at[c])
     dout_slot[c] = dout_t[head_rows, :]
-
-    my_lanes = ds(core * BLK, BLK, BLK)
-    other_half = ds((1 - core) * HALF, HALF, 128)
-    ups = (grad_branch, grad_hidden, cot[...])
-    acts[0, :, my_lanes] = mixed_t[...]
-    acts[1, :, my_lanes] = flip(normed_two)
-    acts[2, :, my_lanes] = flip(active)
-    for w in range(3):
-        up_in[w] = ups[w]
-    give_acts = wire.send(acts.at[:, :, my_lanes], acts.at[:, :, my_lanes], sibling)
-    give_up = wire.send(up_in.at[:, :, other_half], up_all.at[:, my_lanes], sibling)
-    for w in range(3):
-        up_all[w, my_lanes, :] = up_in[w, :, half_cols]
+    shared[0] = share(0, mixed_t[...], grad_branch)
+
+    second_set.third()
+    def scatter(w, stage, src_of, dst_of):
+        return [wire.send(src_of((place(w, stage) + k) % 4), dst_of(k - 1), along(w, stage, k)) for k in range(1, 4)]
+
+    def gathered_sum(w, stage, indices, first, buffers):
+        for k, index in enumerate(indices):
+            wire.receive(index, buffers.at[w, k], along(w, stage, 3 - k))
+        return first.astype(f32) + buffers[w, 0].astype(f32) + buffers[w, 1].astype(f32) + buffers[w, 2].astype(f32)
+
+    stage_one, stage_two, stage_three = {}, {}, {}
+    for w in (2, 1, 0):
+        wire.receive(shared[w][0], acts.at[w, :, sib_lanes], sibling)
+        wire.receive(shared[w][1], up_all.at[w, sib_lanes], sibling)
+        for n in range(0, D, 320):
+            rows = slice(n, n + 320)
+            t1[w, rows, :] = nn(acts[w, rows, :], up_all[w]).astype(bf16)
+        stage_one[w] = scatter(w, 0, lambda d: t1.at[w, ds(d * 320, 320, 320)], lambda k: r1.at[w, k])
+
     layer_out[...] = (after + spread(active, 2) + bias_down).astype(bf16)
     input_grad[...] = grad_after
     ar_own[...] = jnp.zeros_like(ar_own)
     ar_own[1:2, :] = jnp.sum(back_two * n_two, axis=0, keepdims=True)
     ar_own[2:3, :] = jnp.sum(grad_hidden.astype(f32), axis=0, keepdims=True)
     ar_own[3:4, :] = jnp.sum(cot_f, axis=0, keepdims=True)
-
-    second_set.third()
-    sib_lanes = ds((1 - core) * BLK, BLK, BLK)
-    wire.receive(give_acts, acts.at[:, :, sib_lanes], sibling)
-    wire.receive(give_up, up_all.at[:, sib_lanes], sibling)
-
-    def scatter(w, stage, src_of, dst_of):
-        axis = axes[w][stage]
-        return [
-            wire.send(src_of((here[axis] + k) % 4), dst_of(k - 1), away(**{"d" + axis: k})) for k in range(1, 4)
-        ]
-
-    def gathered_sum(w, stage, indices, first, buffers):
-        axis = axes[w][stage]
-        for k, index in enumerate(indices):
-            wire.receive(index, buffers.at[w, k], away(**{"d" + axis: 3 - k}))
-        return first.astype(f32) + buffers[w, 0].astype(f32) + buffers[w, 1].astype(f32) + buffers[w, 2].astype(f32)
-
-    stage_one, stage_two, stage_three = {}, {}, {}
-    for w in (2, 1, 0):
-        for n in range(0, D, 320):
-            rows = slice(n, n + 320)
-            t1[w, rows, :] = nn(acts[w, rows, :], up_all[w]).astype(bf16)
-        stage_one[w] = scatter(w, 0, lambda d: t1.at[w, ds(d * 320, 320, 320)], lambda k: r1.at[w, k])
-
     def second_stage(w):
-        mine = t1[w, ds(here[axes[w][0]] * 320, 320, 320), :]
+        mine = t1[w, ds(place(w, 0) * 320, 320, 320), :]
         t2[w] = gathered_sum(w, 0, stage_one[w], mine, r1).astype(bf16)
         stage_two[w] = scatter(w, 1, lambda d: t2.at[w, ds(d * 80, 80, 80)], lambda k: r2.at[w, k])
 
     def third_stage(w):
-        mine = t2[w, ds(here[axes[w][1]] * 80, 80, 80), :]
+        mine = t2[w, ds(place(w, 1) * 80, 80, 80), :]
         both = gathered_sum(w, 1, stage_two[w], mine, r2)
         for d in range(4):
             t3[w, d] = jnp.concatenate([both[20 * d:20 * d + 20], jnp.zeros((12, HALF), f32)], axis=0).astype(bf16)
         stage_three[w] = scatter(w, 2, lambda d: t3.at[w, d], lambda k: r3.at[w, k])
 
     def fourth_stage(w):
-        both = gathered_sum(w, 2, stage_three[w], t3[w, here[axes[w][2]]], r3)
+        both = gathered_sum(w, 2, stage_three[w], t3[w, place(w, 2)], r3)
+        base = wire.used
+        wire.used += 2
+        copies = []
         for i in range(2):
-            swap_out[w, i] = jnp.concatenate([both[10 * i:10 * i + 10], jnp.zeros((6, HALF), f32)], axis=0)
-        rows_out[w, :, half_cols] = swap_out[w, core]
-        return wire.send(swap_out.at[w, 1 - core], rows_out.at[w, :, half_cols], sibling)
+            rows_out[w, i] = jnp.concatenate([both[10 * i:10 * i + 10], jnp.zeros((6, HALF), f32)], axis=0)
+            target = final_target(w, i)
+            stays = (target[0] == c) & (target[1] == f)
+            to = rows_in.at[w, :, half_cols]
+            copy = pltpu.make_async_remote_copy(
+                src_ref=rows_out.at[w, i], dst_ref=to, send_sem=send_sems.at[base + i],
+                recv_sem=recv_sems.at[base + core], device_id=target, device_id_type=MESH,
+            )
+            within = pltpu.make_async_copy(rows_out.at[w, i], to, recv_sems.at[base + core])
+            pl.when(jnp.logical_not(stays))(copy.start)
+            pl.when(stays)(within.start)
+            copies.append((copy, stays))
+        return w, base, copies
 
     second_set.fourth()
     arrive(douts, lambda src: dout_slot.at[src])
@@ -610,27 +631,17 @@
     through = r_one * (scaled - n_one * jnp.mean(scaled * n_one, axis=1, keepdims=True))
     input_grad[...] = input_grad[...] + through
 
-    swaps = [(w, fourth_stage(w)) for w in (2, 1, 0)]
-    finals = []
-    for w, index in swaps:
-        wire.receive(index, rows_out.at[w, :, other_half], sibling)
-        target = final_target(w)
-        index = wire.used
-        wire.used += 1
-        stays = (target[0] == c) & (target[1] == f)
-        copy = wire.copy(index, rows_out.at[w], rows_in.at[w], target)
-        within = pltpu.make_async_copy(rows_out.at[w], rows_in.at[w], recv_sems.at[index])
-        pl.when(jnp.logical_not(stays))(copy.start)
-        pl.when(stays)(within.start)
-        finals.append((w, index, copy, stays))
+    finals = [fourth_stage(w) for w in (2, 1, 0)]
 
     wire.receive(half_sums, ar_total.at[:, other_half], sibling)
     small_out[...] = ar_total[...]
     arrive(heads, lambda src: gq_in.at[src])
     grad_qkv[...] = gq_in[...]
-    for w, index, copy, stays in finals:
-        wire.receive(index, rows_in.at[w], final_source(w))
-        pl.when(jnp.logical_not(stays))(copy.wait_send)
+    for w, base, copies in finals:
+        for core_at in range(2):
+            wire.receive(base + core_at, rows_in.at[w, :, core_at * HALF:(core_at + 1) * HALF], final_source(w, core_at))
+        for copy, stays in copies:
+            pl.when(jnp.logical_not(stays))(copy.wait_send)
     grad_mlp[...] = rows_in[...]
     wire.drain()
     assert wire.used <= N_SEM
@@ -684,7 +695,7 @@
         "acts": ((3, D, 2 * BLK), bf16), "up_in": ((3, BLK, D), bf16), "up_all": ((3, 2 * BLK, HALF), bf16),
         "t1": ((3, D, HALF), bf16), "r1": ((3, 3, 320, HALF), bf16), "t2": ((3, 320, HALF), bf16),
         "r2": ((3, 3, 80, HALF), bf16), "t3": ((3, 4, 32, HALF), bf16), "r3": ((3, 3, 32, HALF), bf16),
-        "swap_out": ((3, 2, 16, HALF), f32), "rows_out": ((3, 16, D), f32), "rows_in": ((3, 16, D), f32),
+        "rows_out": ((3, 2, 16, HALF), f32), "rows_in": ((3, 16, D), f32),
         "gw": ((D, 256), f32), "gw_send": ((8, SHARD, 256), bf16), "gw_in": ((7, SHARD, 256), bf16),
         "gq_send": ((16, 16, 256), bf16), "gq_in": ((16, 16, 256), bf16),
         "ar_own": ((8, D), f32), "ar_half": ((8, HALF), f32), "ar_slots": ((3, 4, 8, HALF), f32),

time: 154 us -> 150 us (0.974)
  Pallas kernels: 153 us -> 149 us
    pallas_call x1, Pallas kernels: 150 us -> 146 us  [on_device(): pl.pallas_call(body, out_shape=[jax.ShapeDtypeStruct(*s) for s in outs.va...]
where the time goes in v3:
time: 150 us
  Pallas kernels  149 us (99%)
    pallas_call x1, Pallas kernels, on_device(): pl.pallas_call(body, out_shape=[jax.ShapeDtypeStruct(*s) for s in outs.va...  146 us
    pallas_call x1, Pallas kernels, on_device(): pl.pallas_call(outputs, out_shape=[jax.ShapeDtypeStruct((1, BLK, D), bf16...  3.11 us

profile of v3, /device:TPU:24, one launch (start us, length us, event | category | flops | bytes accessed | tf_op | source)
XLA Modules:
  0.0 149.8 jit_solution(17616332687718109616)
XLA Ops:
  0.7 145.9 %shard_map.246 = (bf16[128,1280]{1,0:T(8,128)(2,1)}, f32[128,1280]{1,0:T(8,128)}, f32[3,16,1280]{2,1,0:T(8,128)}, bf16[16,16,256]{2,1,0:T(8,128)(2,1)}, f32[8,12...) custom-call(s32[1,4]{1,0:T(1,128)} %refs_0_.1, s32[1,16]{1,0:T(1,128)} %refs_1_.1, bf16[128,1280]{1,0:T(8,128)(2,1)} %bitcast.2, ...), custom_call_target="tpu_custom_call" | custom-call | tf_op jit(solution)/shard_map/pallas_call | solution.py:717
  146.6 3.1 %shard_map.247 = (bf16[1,128,1280]{2,1,0:T(8,128)(2,1)}, f32[1,128,1280]{2,1,0:T(8,128)}, f32[10,1280]{1,0:T(8,128)}, f32[10,1280]{1,0:T(8,128)}, f32[10,1280]{1...) custom-call(bf16[128,1280]{1,0:T(8,128)(2,1)} %get-tuple-element.18., ...), custom_call_target="tpu_custom_call" | custom-call | tf_op jit(solution)/shard_map/pallas_call | solution.py:733

commit v4 on v3

--- a/solution.py
+++ b/solution.py
@@ -79,7 +79,7 @@
     head_send, mixed_t, dout_t, dout_slot, dout_pos, dk_acc, dv_acc, grads_pos, grads_flat, grads_in,
     acts, up_in, up_all, t1, r1, t2, r2, t3, r3, rows_out, rows_in,
     gw, gw_send, gw_in, gq_send, gq_in, ar_own, ar_half, ar_slots, ar_total,
-    local_sems, send_sems, recv_sems,
+    layer_here, grad_here, local_sems, send_sems, recv_sems,
 ):
     c, f = lax.axis_index("ctx"), lax.axis_index("fsdp")
     y_hi, x, core = c // 8, (c // 2) % 4, c % 2
@@ -486,8 +486,10 @@
             t1[w, rows, :] = nn(acts[w, rows, :], up_all[w]).astype(bf16)
         stage_one[w] = scatter(w, 0, lambda d: t1.at[w, ds(d * 320, 320, 320)], lambda k: r1.at[w, k])
 
-    layer_out[...] = (after + spread(active, 2) + bias_down).astype(bf16)
-    input_grad[...] = grad_after
+    layer_here[...] = (after + spread(active, 2) + bias_down).astype(bf16)
+    grad_here[...] = grad_after
+    put_layer = pltpu.make_async_copy(layer_here, layer_out, local_sems.at[7])
+    put_layer.start()
     ar_own[...] = jnp.zeros_like(ar_own)
     ar_own[1:2, :] = jnp.sum(back_two * n_two, axis=0, keepdims=True)
     ar_own[2:3, :] = jnp.sum(grad_hidden.astype(f32), axis=0, keepdims=True)
@@ -629,7 +631,9 @@
     n_one = x_in * r_one
     scaled = grad_normed * gain_one
     through = r_one * (scaled - n_one * jnp.mean(scaled * n_one, axis=1, keepdims=True))
-    input_grad[...] = input_grad[...] + through
+    grad_here[...] = grad_here[...] + through
+    put_grad = pltpu.make_async_copy(grad_here, input_grad, local_sems.at[8])
+    put_grad.start()
 
     finals = [fourth_stage(w) for w in (2, 1, 0)]
 
@@ -643,6 +647,8 @@
         for copy, stays in copies:
             pl.when(jnp.logical_not(stays))(copy.wait_send)
     grad_mlp[...] = rows_in[...]
+    put_layer.wait()
+    put_grad.wait()
     wire.drain()
     assert wire.used <= N_SEM
 
@@ -650,9 +656,9 @@
 def outputs(
     out, in_grad, rows, qkv, small, q_scale,
     layer_out, input_grad, g_query, g_key, g_value, g_out, g_up, g_down, g_gain_one, g_gain_two, g_scale, g_bias_up, g_bias_down,
-    rows_here, qkv_here, small_here, sems,
+    layer_here, grad_here, rows_here, qkv_here, small_here, sems,
 ):
-    places = (layer_out.at[0], input_grad.at[0], rows_here, qkv_here, small_here)
+    places = (layer_here, grad_here, rows_here, qkv_here, small_here)
     copies = [
         pltpu.make_async_copy(src, dst, sems.at[i]) for i, (src, dst) in enumerate(zip((out, in_grad, rows, qkv, small), places))
     ]
@@ -660,6 +666,12 @@
         copy.start()
     for copy in copies:
         copy.wait()
+    stores = [
+        pltpu.make_async_copy(layer_here, layer_out.at[0], sems.at[5]),
+        pltpu.make_async_copy(grad_here, input_grad.at[0], sems.at[6]),
+    ]
+    for store in stores:
+        store.start()
     rows, qkv, small = rows_here, qkv_here, small_here
     for j, ref in enumerate((g_query, g_key, g_value)):
         tiles = [jnp.zeros((16, BLK), f32) for _ in range(11)]
@@ -676,6 +688,8 @@
     for i, ref in ((0, g_gain_one), (1, g_gain_two), (2, g_bias_up), (3, g_bias_down)):
         ref[...] = small[i, :]
     g_scale[...] = small[4, :HEAD_DIM] * QUERY_CONST * jax.nn.sigmoid(q_scale[...])
+    for store in stores:
+        store.wait()
 
 
 def on_device(
@@ -699,7 +713,7 @@
         "gw": ((D, 256), f32), "gw_send": ((8, SHARD, 256), bf16), "gw_in": ((7, SHARD, 256), bf16),
         "gq_send": ((16, 16, 256), bf16), "gq_in": ((16, 16, 256), bf16),
         "ar_own": ((8, D), f32), "ar_half": ((8, HALF), f32), "ar_slots": ((3, 4, 8, HALF), f32),
-        "ar_total": ((8, D), f32),
+        "ar_total": ((8, D), f32), "layer_here": ((BLK, D), bf16), "grad_here": ((BLK, D), f32),
     }
     outs = {
         "layer_out": ((BLK, D), bf16), "input_grad": ((BLK, D), f32), "grad_mlp": ((3, 16, D), f32),
@@ -718,9 +732,9 @@
         body,
         out_shape=[jax.ShapeDtypeStruct(*s) for s in outs.values()],
         in_specs=[smem, smem] + [vmem] * 2 + [any_space] * 6 + [vmem] * 5,
-        out_specs=[vmem] * (len(outs) - 1) + [any_space],
+        out_specs=[any_space] * 2 + [vmem] * (len(outs) - 3) + [any_space],
         scratch_shapes=[pltpu.VMEM(*s) for s in shapes.values()]
-        + [pltpu.SemaphoreType.DMA((7,)), pltpu.SemaphoreType.DMA((N_SEM,)), pltpu.SemaphoreType.DMA((N_SEM,))],
+        + [pltpu.SemaphoreType.DMA((9,)), pltpu.SemaphoreType.DMA((N_SEM,)), pltpu.SemaphoreType.DMA((N_SEM,))],
         compiler_params=pltpu.CompilerParams(
             collective_id=0, has_side_effects=True, vmem_limit_bytes=62 << 20
         ),
@@ -737,10 +751,11 @@
             vector, vector, jax.ShapeDtypeStruct((HEAD_DIM,), f32), vector, vector,
         ],
         in_specs=[any_space] * 5 + [vmem],
-        out_specs=[vmem] * 13,
+        out_specs=[any_space] * 2 + [vmem] * 11,
         scratch_shapes=[
+            pltpu.VMEM((BLK, D), bf16), pltpu.VMEM((BLK, D), f32),
             pltpu.VMEM((3, 16, D), f32), pltpu.VMEM((16, 16, 256), bf16), pltpu.VMEM((8, D), f32),
-            pltpu.SemaphoreType.DMA((5,)),
+            pltpu.SemaphoreType.DMA((7,)),
         ],
         compiler_params=pltpu.CompilerParams(vmem_limit_bytes=62 << 20),
     )(out, in_grad, rows, qkv, small, q_scale)

time: 150 us -> 150 us (level)
  no operation moved by 1% of the time
where the time goes in v4:
time: 150 us
  Pallas kernels  149 us (99%)
    pallas_call x1, Pallas kernels, on_device(): pl.pallas_call(body, out_shape=[jax.ShapeDtypeStruct(*s) for s in outs.va...  146 us
    pallas_call x1, Pallas kernels, on_device(): pl.pallas_call(outputs, out_shape=[jax.ShapeDtypeStruct((1, BLK, D), bf16...  3.73 us

profile of v4, /device:TPU:24, one launch (start us, length us, event | category | flops | bytes accessed | tf_op | source)
XLA Modules:
  0.0 150.2 jit_solution(4407778405217138837)
XLA Ops:
  0.7 145.7 %shard_map.246 = (bf16[128,1280]{1,0:T(8,128)(2,1)}, f32[128,1280]{1,0:T(8,128)}, f32[3,16,1280]{2,1,0:T(8,128)}, bf16[16,16,256]{2,1,0:T(8,128)(2,1)}, f32[8,12...) custom-call(s32[1,4]{1,0:T(1,128)} %refs_0_.1, s32[1,16]{1,0:T(1,128)} %refs_1_.1, bf16[128,1280]{1,0:T(8,128)(2,1)} %bitcast.2, ...), custom_call_target="tpu_custom_call" | custom-call | tf_op jit(solution)/shard_map/pallas_call | solution.py:731
  146.3 3.7 %shard_map.247 = (bf16[1,128,1280]{2,1,0:T(8,128)(2,1)}, f32[1,128,1280]{2,1,0:T(8,128)}, f32[10,1280]{1,0:T(8,128)}, f32[10,1280]{1,0:T(8,128)}, f32[10,1280]{1...) custom-call(bf16[128,1280]{1,0:T(8,128)(2,1)} %get-tuple-element.18., ...), custom_call_target="tpu_custom_call" | custom-call | tf_op jit(solution)/shard_map/pallas_call | solution.py:747
